TPU v7x, 512 devices: a whole 4x8x8 slice. The times are simulated.
512 devices in a mesh: sector: 64 (over y, z), axial: 8 (over x, core).
Axes of the slice: x: 4, y: 8, z: 8, core: 2. Of those that a mesh axis runs over, the one named last changes fastest.
Arguments:
- right_side: float32 [16, 32, 8192], P(None, 'axial', 'sector'), may hold values from -6 to 6
- mass_term: float32 [32, 8192], P('axial', 'sector'), may hold values from 0.05 to 2
- band_weight: float32 [8, 8192], P('axial', 'sector'), may hold values from 0.5 to 2
- band_shift: int32 [1], replicated, may hold values from 1 to 63
- local_solver: bfloat16 [8, 32768, 780], P('axial', 'sector'), may hold values from -0.25 to 0.25
- coarse_inverse: bfloat16 [8192, 8192], P(('sector', 'axial')), may hold values from -1 to 1
- coarse_basis: bfloat16 [16, 32, 8192], P(None, 'axial', 'sector'), may hold values from -0.25 to 0.25
Outputs:
- solution: float32 [16, 32, 8192], P(None, 'axial', 'sector')
- residual: float32 [16, 32, 8192], P(None, 'axial', 'sector')
All inputs are finite; a program needn't handle non-finite values.
Results may differ from a plain program's by a relative error of at most 0.0027.
Values may be sent and summed in bfloat16 or wider, within the bound.
A program may use at most 64 MiB of HBM per device.

v0:
```python
import jax
import jax.numpy as jnp
from jax import lax
from jax.sharding import PartitionSpec as P

ITERS = 2


TOPMOST_ACCURACY = lax.Precision.HIGHEST
EPSILON = 1e-06


def with_halo(array, sides, width):
    for axis, dim in sides:
        size, length = (lax.axis_size(axis), array.shape[dim])
        up = [(i, (i + 1) % size) for i in range(size)]
        down = [(j, i) for i, j in up]
        last = lax.slice_in_dim(array, length - width, length, axis=dim)
        first = lax.slice_in_dim(array, 0, width, axis=dim)
        before = lax.ppermute(last, axis, up)
        after = lax.ppermute(first, axis, down)
        array = jnp.concatenate([before, array, after], axis=dim)
    return array


def on_device(
    right_side, mass_term, band_weight, band_shift, local_solver, coarse_inverse, coarse_basis
):
    rhs_count = right_side.shape[0]
    rows_own = right_side.shape[1]
    cols_own = right_side.shape[2]
    basis_single_float32 = coarse_basis.astype(jnp.float32)
    inverse_rows = coarse_inverse.astype(jnp.float32)
    solver_rows = local_solver[0]
    axial_location = lax.axis_index("axial")
    axial_count = lax.axis_size("axial")
    sector_pos = lax.axis_index("sector")
    sector_count = lax.axis_size("sector")
    shift_value = band_shift[0]
    row_index = lax.broadcasted_iota(jnp.int32, (rows_own + 2, cols_own + 2), 0)
    col_index = lax.broadcasted_iota(jnp.int32, (rows_own + 2, cols_own + 2), 1)
    corner = ((row_index == 0) | (row_index == rows_own + 1)) & (
        (col_index == 0) | (col_index == cols_own + 1)
    )
    lower_end = (row_index == 0) & (axial_location == 0)
    upper_end = (row_index == rows_own + 1) & (axial_location == axial_count - 1)
    keep_mask = jnp.logical_not(corner | lower_end | upper_end)
    solution = jnp.zeros_like(right_side)
    residual = right_side
    for sweep in range(ITERS):
        coarse_combined = lax.all_gather(
            jnp.einsum("lds,kds->lk", residual, basis_single_float32, precision=TOPMOST_ACCURACY),
            ("sector", "axial"),
            axis=1,
            tiled=True,
        )
        rounded = residual.astype(jnp.bfloat16)
        padded = with_halo(rounded, (("sector", 2), ("axial", 1)), 1)
        window = jnp.where(keep_mask[None], padded, jnp.zeros((), jnp.bfloat16)).reshape(
            rhs_count, -1
        )
        local_part = lax.dot_general(
            window, solver_rows, (((1,), (1,)), ((), ())), preferred_element_type=jnp.float32
        )
        coarse_answer = lax.dot_general(
            coarse_combined, inverse_rows, (((1,), (1,)), ((), ())), precision=TOPMOST_ACCURACY
        )
        correction = local_part.reshape(rhs_count, rows_own, cols_own) + jnp.einsum(
            "sj,jyz->syz", coarse_answer, basis_single_float32, precision=TOPMOST_ACCURACY
        )
        extend_padded = with_halo(correction, (("sector", 2), ("axial", 1)), 1)
        operate_padded = jnp.where(keep_mask[None], extend_padded, 0.0)
        beside = operate_padded[:, 2:, 1:-1] + operate_padded[:, :-2, 1:-1]
        beside = beside + operate_padded[:, 1:-1, 2:] + operate_padded[:, 1:-1, :-2]
        result = (4.0 + mass_term)[None] * correction - beside
        operate_band_row = correction[:, 0, :]
        gathered = lax.all_gather(operate_band_row, "sector", axis=1, tiled=True)
        source = (sector_pos - shift_value) % sector_count
        band_term = band_weight[0][None] * (
            operate_band_row - lax.dynamic_slice_in_dim(gathered, source * cols_own, cols_own, 1)
        )
        image_field = result.at[:, 0, :].add(band_term)
        part_cross = jnp.sum(residual * image_field, axis=(1, 2))
        part_square = jnp.sum(image_field * image_field, axis=(1, 2))
        cross_sum, square_sum = lax.psum((part_cross, part_square), ("sector", "axial"))
        step_len = cross_sum / (square_sum + EPSILON)
        solution = solution + step_len[:, None, None] * correction
        residual = residual - step_len[:, None, None] * image_field
    return (solution, residual)


def solution(mesh):
    placed = (
        P(None, "axial", "sector"),
        P("axial", "sector"),
        P("axial", "sector"),
        P(),
        P("axial", "sector", None),
        P(("sector", "axial"), None),
        P(None, "axial", "sector"),
    )
    return jax.shard_map(
        on_device,
        mesh=mesh,
        in_specs=placed,
        out_specs=(P(None, "axial", "sector"), P(None, "axial", "sector")),
        check_vma=False,
    )
```

profile of v0, /device:TPU:1, one launch (start us, length us, event | category | flops | bytes accessed | tf_op | source)
XLA Modules:
  0.0 510.9 jit_solution(7516394156516160319)
XLA Ops:
  0.7 0.8 copy.66
  1.5 14.4 %collective-permute-start.1 = (bf16[16,4,1]{2,0,1:T(8,128)(2,1)S(1)}, bf16[16,4,1]{2,0,1:T(8,128)(2,1)S(1)}, u32[]{:S(2)}, u32[]{:S(2)}) collective-permute-start(bf16[16,4,1]{2,0,1:T(8,128)(2,1)S(1)} %get-tuple-element.57), channel_id=1, source_target_pairs={{8,0},{16,8},{24,16},{32,24},{40,32},{48,40},{56,48},{64,56},{72,6... | collective-permute-start | bytes 392 | tf_op jit(solution)/shard_map/ppermute | solution.py:21
  15.9 1.9 collective-permute-start
  17.9 0.9 convolution_bitcast_fusion.1
  18.8 78.0 %all_gather.12 = f32[16,8192]{0,1:T(8,128)S(1)} all-gather(f32[16,16]{0,1:T(8,128)S(1)} %convolution_bitcast_fusion.1), channel_id=1, replica_groups=mesh['sector'=64,'axial'=8] {'sector','axial'}, dimensions={1}, use_global_device_ids=true | all-gather | bytes 525312 | tf_op jit(solution)/shard_map/all_gather | solution.py:51
  96.8 3.5 convolution_bitcast_fusion.3
  100.6 1.6 collective-permute-start.2
  102.9 0.3 dot_general.26
  103.2 0.3 collective-permute-done.3
  103.9 0.2 fusion.2
  104.1 0.1 convolution_add_fusion.1
  104.3 4.3 collective-permute-start.5
  108.6 1.9 collective-permute-start.4
  110.6 6.0 %collective-permute-done.4 = f32[16,4,1]{2,0,1:T(8,128)S(1)} collective-permute-done((f32[16,4,1]{2,0,1:T(8,128)S(1)}, f32[16,4,1]{2,0,1:T(8,128)S(1)}, u32[]{:S(2)}, u32[]{:S(2)}) %collective-permute-start.4) | collective-permute-done | bytes 288 | tf_op jit(solution)/shard_map/ppermute | solution.py:20
  116.7 5.1 collective-permute-start.7
  121.7 34.3 %all-gather = f32[16,1,8192]{2,0,1:T(8,128)S(1)} all-gather(f32[16,1,128]{2,0,1:T(8,128)S(1)} %slice.159), channel_id=2, replica_groups=mesh['sector'=64,'axial'=8] {'sector'}, dimensions={2}, use_global_device_ids=true | all-gather | bytes 532480 | tf_op jit(solution)/shard_map/all_gather | solution.py:77
  156.4 107.1 %all-reduce.1 = (f32[16]{0:T(128)S(1)}, f32[16]{0:T(128)S(1)}) all-reduce(f32[16]{0:T(128)S(1)} %get-tuple-element.35, f32[16]{0:T(128)S(1)} %get-tuple-element.34), channel_id=1, replica_groups=mesh['sector'=64,'axial'=8] {'sector','axial'}, use_global_device_ids=true, to_apply=%region_1.2 | all-reduce | flops 32 | bytes 256 | tf_op jit(solution)/shard_map/psum | solution.py:85
  263.7 3.1 collective-permute-start.9
  266.8 2.2 collective-permute-start.8
  269.1 77.4 %all_gather.14 = f32[16,8192]{0,1:T(8,128)S(1)} all-gather(f32[16,16]{0,1:T(8,128)S(1)} %convolution_bitcast_fusion), channel_id=1, replica_groups=mesh['sector'=64,'axial'=8] {'sector','axial'}, dimensions={1}, use_global_device_ids=true | all-gather | bytes 525312 | tf_op jit(solution)/shard_map/all_gather | solution.py:51
  346.6 0.1 collective-permute-start.11
  346.7 1.6 collective-permute-start.10
  348.4 3.5 convolution_bitcast_fusion.2
  352.1 0.2 fusion
  352.5 4.3 collective-permute-start.13
  356.9 1.9 collective-permute-start.12
  358.8 6.0 %collective-permute-done.12 = f32[16,4,1]{2,0,1:T(8,128)S(1)} collective-permute-done((f32[16,4,1]{2,0,1:T(8,128)S(1)}, f32[16,4,1]{2,0,1:T(8,128)S(1)}, u32[]{:S(2)}, u32[]{:S(2)}) %collective-permute-start.12) | collective-permute-done | bytes 288 | tf_op jit(solution)/shard_map/ppermute | solution.py:20
  364.9 2.6 collective-permute-start.15
  367.6 34.6 %all-gather.1 = f32[16,1,8192]{2,0,1:T(8,128)S(1)} all-gather(f32[16,1,128]{2,0,1:T(8,128)S(1)} %slice.169), channel_id=3, replica_groups=mesh['sector'=64,'axial'=8] {'sector'}, dimensions={2}, use_global_device_ids=true | all-gather | bytes 532480 | tf_op jit(solution)/shard_map/all_gather | solution.py:77
  402.5 107.1 %all-reduce = (f32[16]{0:T(128)S(1)}, f32[16]{0:T(128)S(1)}) all-reduce(f32[16]{0:T(128)S(1)} %get-tuple-element.33, f32[16]{0:T(128)S(1)} %get-tuple-element.32), channel_id=1, replica_groups=mesh['sector'=64,'axial'=8] {'sector','axial'}, use_global_device_ids=true, to_apply=%region_5.6 | all-reduce | flops 32 | bytes 256 | tf_op jit(solution)/shard_map/psum | solution.py:85
  509.7 0.6 copy.43
  510.3 0.6 copy.44
  (63 shorter events, 2.6 us)
Async XLA Ops:
  0.6 96.2 %copy-start = (bf16[16,8192]{1,0:T(8,128)(2,1)S(1)}, bf16[16,8192]{1,0:T(8,128)(2,1)}, u32[]{:S(2)}) copy-start(bf16[16,8192]{1,0:T(8,128)(2,1)} %param.16) | copy-start | bytes 786436
  0.6 96.1 %copy-start.5 = (f32[4,128]{1,0:T(4,128)S(1)}, f32[4,128]{1,0:T(4,128)}, u32[]{:S(2)}) copy-start(f32[4,128]{1,0:T(4,128)} %param.12) | copy-start | bytes 6148
  1.5 98.8 %collective-permute-start.1 = (bf16[16,4,1]{2,0,1:T(8,128)(2,1)S(1)}, bf16[16,4,1]{2,0,1:T(8,128)(2,1)S(1)}, u32[]{:S(2)}, u32[]{:S(2)}) collective-permute-start(bf16[16,4,1]{2,0,1:T(8,128)(2,1)S(1)} %get-tuple-element.57), channel_id=1, source_target_pairs={{8,0},{16,8},{24,16},{32,24},{40,32},{48,40},{56,48},{64,56},{72,6... | collective-permute-start | bytes 392 | tf_op jit(solution)/shard_map/ppermute | solution.py:21
  15.9 84.4 %collective-permute-start = (bf16[16,4,1]{2,0,1:T(8,128)(2,1)S(1)}, bf16[16,4,1]{2,0,1:T(8,128)(2,1)S(1)}, u32[]{:S(2)}, u32[]{:S(2)}) collective-permute-start(bf16[16,4,1]{2,0,1:T(8,128)(2,1)S(1)} %get-tuple-element.56), channel_id=1, source_target_pairs={{0,8},{8,16},{16,24},{24,32},{32,40},{40,48},{48,56},{56,64},{64,7... | collective-permute-start | bytes 392 | tf_op jit(solution)/shard_map/ppermute | solution.py:20
  18.8 84.1 %copy-start.1 = (bf16[1,512,780]{1,2,0:T(8,128)(2,1)S(1)}, bf16[1,512,780]{1,2,0:T(8,128)(2,1)}, u32[]{:S(2)}) copy-start(bf16[1,512,780]{1,2,0:T(8,128)(2,1)} %param.15) | copy-start | bytes 2396164
  96.8 7.3 %copy-start.3 = (bf16[16,4,128]{2,1,0:T(4,128)(2,1)S(1)}, bf16[16,4,128]{2,1,0:T(4,128)(2,1)}, u32[]{:S(2)}) copy-start(bf16[16,4,128]{2,1,0:T(4,128)(2,1)} %param.17) | copy-start | bytes 49156
  96.8 59.5 %copy-start.4 = (f32[1,128]{1,0:T(1,128)S(1)}, f32[1,128]{1,0:T(1,128)}, u32[]{:S(2)}) copy-start(f32[1,128]{1,0:T(1,128)} %param.13) | copy-start | bytes 1540
  96.8 59.5 %copy-start.2 = (f32[16,4,128]{2,1,0:T(4,128)S(1)}, f32[16,4,128]{2,1,0:T(4,128)}, u32[]{:S(2)}) copy-start(f32[16,4,128]{2,1,0:T(4,128)} %param.11) | copy-start | bytes 98308
  100.4 3.1 collective-permute-start.3
  100.6 3.1 collective-permute-start.2
  104.3 6.3 %collective-permute-start.5 = (f32[16,4,1]{2,0,1:T(8,128)S(1)}, f32[16,4,1]{2,0,1:T(8,128)S(1)}, u32[]{:S(2)}, u32[]{:S(2)}) collective-permute-start(f32[16,4,1]{2,0,1:T(8,128)S(1)} %get-tuple-element.53), channel_id=1, source_target_pairs={{8,0},{16,8},{24,16},{32,24},{40,32},{48,40},{56,48},{64,56},{72,6... | collective-permute-start | bytes 776 | tf_op jit(solution)/shard_map/ppermute | solution.py:21
  108.6 8.0 %collective-permute-start.4 = (f32[16,4,1]{2,0,1:T(8,128)S(1)}, f32[16,4,1]{2,0,1:T(8,128)S(1)}, u32[]{:S(2)}, u32[]{:S(2)}) collective-permute-start(f32[16,4,1]{2,0,1:T(8,128)S(1)} %get-tuple-element.52), channel_id=1, source_target_pairs={{0,8},{8,16},{16,24},{24,32},{32,40},{40,48},{48,56},{56,64},{64,7... | collective-permute-start | bytes 776 | tf_op jit(solution)/shard_map/ppermute | solution.py:20
  116.7 39.4 %collective-permute-start.7 = (f32[16,1,130]{2,0,1:T(8,128)S(1)}, f32[16,1,130]{2,0,1:T(8,128)S(1)}, u32[]{:S(2)}, u32[]{:S(2)}) collective-permute-start(f32[16,1,130]{2,0,1:T(8,128)S(1)} %get-tuple-element.45), channel_id=1, source_target_pairs={{1,0},{2,1},{3,2},{4,3},{5,4},{6,5},{7,6},{0,7},{9,8},{10,9},{11,1... | collective-permute-start | bytes 24968 | tf_op jit(solution)/shard_map/ppermute | solution.py:21
  121.7 34.3 %collective-permute-start.6 = (f32[16,1,130]{2,0,1:T(8,128)S(1)}, f32[16,1,130]{2,0,1:T(8,128)S(1)}, u32[]{:S(2)}, u32[]{:S(2)}) collective-permute-start(f32[16,1,130]{2,0,1:T(8,128)S(1)} %get-tuple-element.44), channel_id=1, source_target_pairs={{0,1},{1,2},{2,3},{3,4},{4,5},{5,6},{6,7},{7,0},{8,9},{9,10},{10,1... | collective-permute-start | bytes 24968 | tf_op jit(solution)/shard_map/ppermute | solution.py:20
  263.7 82.8 %collective-permute-start.9 = (bf16[16,4,1]{2,0,1:T(8,128)(2,1)S(1)}, bf16[16,4,1]{2,0,1:T(8,128)(2,1)S(1)}, u32[]{:S(2)}, u32[]{:S(2)}) collective-permute-start(bf16[16,4,1]{2,0,1:T(8,128)(2,1)S(1)} %get-tuple-element.55), channel_id=1, source_target_pairs={{8,0},{16,8},{24,16},{32,24},{40,32},{48,40},{56,48},{64,56},{72,6... | collective-permute-start | bytes 392 | tf_op jit(solution)/shard_map/ppermute | solution.py:21
  266.8 79.8 %collective-permute-start.8 = (bf16[16,4,1]{2,0,1:T(8,128)(2,1)S(1)}, bf16[16,4,1]{2,0,1:T(8,128)(2,1)S(1)}, u32[]{:S(2)}, u32[]{:S(2)}) collective-permute-start(bf16[16,4,1]{2,0,1:T(8,128)(2,1)S(1)} %get-tuple-element.54), channel_id=1, source_target_pairs={{0,8},{8,16},{16,24},{24,32},{32,40},{40,48},{48,56},{56,64},{64,7... | collective-permute-start | bytes 392 | tf_op jit(solution)/shard_map/ppermute | solution.py:20
  346.6 5.3 %collective-permute-start.11 = (bf16[16,1,130]{2,0,1:T(8,128)(2,1)S(1)}, bf16[16,1,130]{2,0,1:T(8,128)(2,1)S(1)}, u32[]{:S(2)}, u32[]{:S(2)}) collective-permute-start(bf16[16,1,130]{2,0,1:T(8,128)(2,1)S(1)} %get-tuple-element.47), channel_id=1, source_target_pairs={{1,0},{2,1},{3,2},{4,3},{5,4},{6,5},{7,6},{0,7},{9,8},{10,9},{11,1... | collective-permute-start | bytes 12488 | tf_op jit(solution)/shard_map/ppermute | solution.py:21
  346.7 5.1 %collective-permute-start.10 = (bf16[16,1,130]{2,0,1:T(8,128)(2,1)S(1)}, bf16[16,1,130]{2,0,1:T(8,128)(2,1)S(1)}, u32[]{:S(2)}, u32[]{:S(2)}) collective-permute-start(bf16[16,1,130]{2,0,1:T(8,128)(2,1)S(1)} %get-tuple-element.46), channel_id=1, source_target_pairs={{0,1},{1,2},{2,3},{3,4},{4,5},{5,6},{6,7},{7,0},{8,9},{9,10},{10,1... | collective-permute-start | bytes 12488 | tf_op jit(solution)/shard_map/ppermute | solution.py:20
  352.5 6.3 %collective-permute-start.13 = (f32[16,4,1]{2,0,1:T(8,128)S(1)}, f32[16,4,1]{2,0,1:T(8,128)S(1)}, u32[]{:S(2)}, u32[]{:S(2)}) collective-permute-start(f32[16,4,1]{2,0,1:T(8,128)S(1)} %get-tuple-element.51), channel_id=1, source_target_pairs={{8,0},{16,8},{24,16},{32,24},{40,32},{48,40},{56,48},{64,56},{72,6... | collective-permute-start | bytes 776 | tf_op jit(solution)/shard_map/ppermute | solution.py:21
  356.9 8.0 %collective-permute-start.12 = (f32[16,4,1]{2,0,1:T(8,128)S(1)}, f32[16,4,1]{2,0,1:T(8,128)S(1)}, u32[]{:S(2)}, u32[]{:S(2)}) collective-permute-start(f32[16,4,1]{2,0,1:T(8,128)S(1)} %get-tuple-element.50), channel_id=1, source_target_pairs={{0,8},{8,16},{16,24},{24,32},{32,40},{40,48},{48,56},{56,64},{64,7... | collective-permute-start | bytes 776 | tf_op jit(solution)/shard_map/ppermute | solution.py:20
  364.9 37.2 %collective-permute-start.15 = (f32[16,1,130]{2,0,1:T(8,128)S(1)}, f32[16,1,130]{2,0,1:T(8,128)S(1)}, u32[]{:S(2)}, u32[]{:S(2)}) collective-permute-start(f32[16,1,130]{2,0,1:T(8,128)S(1)} %get-tuple-element.43), channel_id=1, source_target_pairs={{1,0},{2,1},{3,2},{4,3},{5,4},{6,5},{7,6},{0,7},{9,8},{10,9},{11,1... | collective-permute-start | bytes 24968 | tf_op jit(solution)/shard_map/ppermute | solution.py:21
  367.6 34.6 %collective-permute-start.14 = (f32[16,1,130]{2,0,1:T(8,128)S(1)}, f32[16,1,130]{2,0,1:T(8,128)S(1)}, u32[]{:S(2)}, u32[]{:S(2)}) collective-permute-start(f32[16,1,130]{2,0,1:T(8,128)S(1)} %get-tuple-element.42), channel_id=1, source_target_pairs={{0,1},{1,2},{2,3},{3,4},{4,5},{5,6},{6,7},{7,0},{8,9},{9,10},{10,1... | collective-permute-start | bytes 24968 | tf_op jit(solution)/shard_map/ppermute | solution.py:20
where the time goes:
time: 512 us; the launch traced here: 511 us
  blocking collectives  438 us (86%)
  starting transfers between devices  45.2 us (9%)
  waiting for transfers between devices  12.5 us (2%)
  matrix products  8.72 us (2%)
    psum x2, blocking collectives, on_device(): lax.psum((part_cross, part_square), ('sector', 'axial'))  214 us
    all_gather x2, blocking collectives, on_device(): lax.all_gather(jnp.einsum('lds,kds->lk', residual, basis_single_float32,...  155 us
    all_gather x2, blocking collectives, on_device(): gathered = lax.all_gather(operate_band_row, 'sector', axis=1, tiled=True)  68.9 us
    ppermute x8, starting transfers between devices, with_halo(): after = lax.ppermute(first, axis, down)  34 us
    ppermute x8, waiting for transfers between devices, with_halo(): before = lax.ppermute(last, axis, up)  12.2 us
    ppermute x8, starting transfers between devices, with_halo(): before = lax.ppermute(last, axis, up)  11.2 us
  transfers between devices with their start and end apart: 16, of which 4 were waited for; matrix products, arithmetic and copies ran while one was open for 2% of the time, Pallas kernels for 0%

commit v1 on v0

v1 whole, which is shorter than its diff:
```python
import jax
import jax.numpy as jnp
from jax import lax
from jax.experimental import pallas as pl
from jax.experimental.pallas import tpu as pltpu
from jax.sharding import PartitionSpec as P

EPSILON = 1e-06
MESH = pl.DeviceIdType.MESH
F32 = jnp.float32
BF16 = jnp.bfloat16

R = 16
GA = 4
GS = 128
NV = 16
NEXT = 780
NZ = 8
NY = 8
NSEC = NY * NZ
NAX = 8
YROWS = 3 * R
XROWS = 2 * R


def nt(a, b):
    return lax.dot_general(a, b, (((1,), (1,)), ((), ())), preferred_element_type=F32)


def nn(a, b):
    return lax.dot_general(a, b, (((1,), (0,)), ((), ())), preferred_element_type=F32)


def two_parts(x):
    high = x.astype(BF16)
    low = (x - high.astype(F32)).astype(BF16)
    return jnp.concatenate([high, low], axis=0)


def joined(x):
    half = x.shape[0] // 2
    return x[:half] + x[half:]


def body(
    rhs_ref, mass_ref, bw_ref, shift_ref, basis_ref, solver_hbm, inverse_hbm,
    sol_ref, res_ref,
    solver, turned, h_send, h_recv, x_send, x_recv, y_send, y_recv, z_send, z_recv,
    b1_first, b1_second, b2_first, b2_second, tiles,
    local_sems, t_ssem, t_rsem, h_ssem, h_rsem, x_ssem, x_rsem, y_ssem, y_rsem,
    z_ssem, z_rsem, b1_ssem, b1_rsem, b2_ssem, b2_rsem,
):
    b1s = (b1_first, b1_second)
    b2s = (b2_first, b2_second)
    s = lax.axis_index("sector")
    q = lax.axis_index("axial")
    y = s // NZ
    z = s % NZ

    def x_peer(k):
        return (s, (q + k) % NAX)

    def y_peer(k):
        return (((y + k) % NY) * NZ + z, q)

    def z_peer(k):
        return (y * NZ + (z + k) % NZ, q)

    def s_peer(k):
        return ((s + k) % NSEC, q)

    def wait_for(ref, sem):
        pltpu.make_async_copy(ref, ref, sem).wait()

    def remote(src, dst, ssem, rsem, device):
        pltpu.make_async_remote_copy(
            src_ref=src, dst_ref=dst, send_sem=ssem, recv_sem=rsem,
            device_id=device, device_id_type=MESH,
        ).start()

    solver_copy = pltpu.make_async_copy(solver_hbm.at[0], solver, local_sems.at[0])
    solver_copy.start()
    own_copy = pltpu.make_async_copy(
        inverse_hbm.at[:, pl.ds(pl.multiple_of(s * GS, GS), GS)], turned.at[NSEC - 1], local_sems.at[1]
    )
    own_copy.start()

    barrier = pltpu.get_barrier_semaphore()

    def greet(k, carry):
        pl.semaphore_signal(barrier, inc=1, device_id=s_peer(k), device_id_type=MESH)
        return carry

    lax.fori_loop(1, NSEC, greet, 0)
    for k in range(1, NAX):
        pl.semaphore_signal(barrier, inc=1, device_id=x_peer(k), device_id_type=MESH)

    lane = lax.broadcasted_iota(jnp.int32, (R, GS), 1)
    rows128 = lax.broadcasted_iota(jnp.int32, (NAX * NV, GS), 0) // NV
    rhs = rhs_ref[...]
    r0 = [rhs[:, a, :] for a in range(GA)]
    basis_all = basis_ref[...].astype(F32)
    basis = [basis_all[:, a, :] for a in range(GA)]
    mass = [mass_ref[a : a + 1, :] + 4.0 for a in range(GA)]
    weight = bw_ref[...]
    shift = shift_ref[0]
    shift_y = shift // NZ
    shift_z = shift % NZ

    def spread(tile, at):
        return jnp.where(rows128 == at, jnp.concatenate([tile] * 8, axis=0), 0.0).astype(BF16)

    basis_q = jnp.concatenate([spread(t, q) for t in basis], axis=1)
    basis_z = jnp.concatenate([spread(t, z) for t in basis], axis=1)

    def coarse_of(field):
        return joined(nt(two_parts(jnp.concatenate(field, axis=1)), basis_q))

    def edges(field):
        tile = jnp.zeros((R, GS), F32)
        for a in range(GA):
            at = 2 * (a + 1)
            tile = jnp.where(lane == at, pltpu.roll(field[a], at + 1, 1), tile)
            tile = jnp.where(lane == at + 1, pltpu.roll(field[a], at + 1, 1), tile)
        return tile

    def send_halo(n, field):
        h_send[n, 0] = edges(field)
        h_send[n, 1] = field[0]
        h_send[n, 2] = field[GA - 1]
        remote(h_send.at[n, 2], h_recv.at[n, 2], h_ssem.at[n], h_rsem.at[n], x_peer(1))
        remote(h_send.at[n, 1], h_recv.at[n, 3], h_ssem.at[n], h_rsem.at[n], x_peer(NAX - 1))
        remote(h_send.at[n, 0], h_recv.at[n, 0], h_ssem.at[n], h_rsem.at[n], s_peer(1))
        remote(h_send.at[n, 0], h_recv.at[n, 1], h_ssem.at[n], h_rsem.at[n], s_peer(NSEC - 1))

    def get_halo(n):
        wait_for(h_recv.at[n], h_rsem.at[n])
        above = jnp.where(q == 0, 0.0, h_recv[n, 2])
        below = jnp.where(q == NAX - 1, 0.0, h_recv[n, 3])
        return h_recv[n, 0], h_recv[n, 1], above, below

    def local_solve(field, halo):
        left, right, above, below = halo
        stack = [above] + field + [below]
        turned_rows = [pltpu.roll(stack[j], 2 * j + 1, 1) for j in range(GA + 2)]
        zero = jnp.zeros((R, GS), F32)
        parts = []
        for t in range(GA + 3):
            here = turned_rows[t] if t < GA + 2 else zero
            before = turned_rows[t - 1] if t > 0 else zero
            tile = jnp.where(lane == 2 * t - 1, right, before)
            tile = jnp.where(lane == 2 * t, left, tile)
            parts.append(jnp.where(lane > 2 * t, here, tile))
        window = jnp.concatenate(parts, axis=1)
        out = joined(nt(two_parts(window)[:, :NEXT], solver[...]))
        return [out[:, a * GS : (a + 1) * GS] for a in range(GA)]

    def apply_operator(field, halo, band):
        left, right, above, below = halo
        stack = [above] + field + [below]
        image = []
        for a in range(GA):
            u = field[a]
            before = jnp.where(lane == 0, pltpu.roll(left, GS - 2 * (a + 1), 1), pltpu.roll(u, 1, 1))
            after = jnp.where(
                lane == GS - 1, pltpu.roll(right, GS - 1 - (2 * a + 3), 1), pltpu.roll(u, GS - 1, 1)
            )
            value = mass[a] * u - ((stack[a + 2] + stack[a]) + before + after)
            if a == 0:
                value = value + weight * (u - band)
            image.append(value)
        return image

    def send_band(n, rows):
        b1s[n][0] = rows
        for k in range(1, NZ):
            remote(b1s[n].at[0], b1s[n].at[k], b1_ssem.at[n], b1_rsem.at[n], s_peer(k))

    def forward_band(n):
        wait_for(b1s[n].at[pl.ds(1, NZ - 1)], b1_rsem.at[n])
        b2s[n][0] = b1s[n][shift_z]
        for k in range(1, NY):
            remote(b2s[n].at[0], b2s[n].at[k], b2_ssem.at[n], b2_rsem.at[n], y_peer(k))

    def get_band(n):
        wait_for(b2s[n].at[pl.ds(1, NY - 1)], b2_rsem.at[n])
        return b2s[n][shift_y]

    def send_x(n, coarse, inner):
        x_send[n, pl.ds(0, R)] = coarse
        x_send[n, pl.ds(R, R)] = inner
        for k in range(1, NAX):
            remote(x_send.at[n], x_recv.at[n, k - 1], x_ssem.at[n], x_rsem.at[n], x_peer(k))

    def get_x(n):
        wait_for(x_recv.at[n], x_rsem.at[n])
        total = x_send[n]
        for k in range(NAX - 1):
            total = total + x_recv[n, k]
        return total[:R], total[R:]

    def send_y(n, coarse, inner):
        out = joined(nt(two_parts(coarse), turned_matrix))
        rolled = []
        for t in range(NY):
            tile = out[:, t * GS : (t + 1) * GS]
            y_send[n, t, pl.ds(0, R)] = tile
            y_send[n, t, pl.ds(2 * R, R)] = inner
            tiles[t] = pltpu.roll(tile, shift_z * NV, 1)
        for t in range(NY):
            here = tiles[(t + NY - shift_y) % NY]
            before = tiles[(t + NY - 1 - shift_y) % NY]
            y_send[n, t, pl.ds(R, R)] = jnp.where(lane >= shift_z * NV, here, before)
        for k in range(1, NY):
            remote(
                y_send.at[n, (y + k) % NY], y_recv.at[n, k - 1], y_ssem.at[n], y_rsem.at[n], y_peer(k)
            )

    def pass_z(n):
        wait_for(y_recv.at[n], y_rsem.at[n])
        total = y_send[n, y]
        for k in range(NY - 1):
            total = total + y_recv[n, k]
        z_send[n] = total
        for k in range(1, NZ):
            remote(z_send.at[n], z_recv.at[n, k - 1], z_ssem.at[n], z_rsem.at[n], z_peer(k))

    def get_z(n):
        wait_for(z_recv.at[n], z_rsem.at[n])
        total = z_send[n]
        for k in range(NZ - 1):
            total = total + z_recv[n, k]
        return total[:R], total[R : 2 * R], total[2 * R :]

    def prolong(coarse, rows):
        out = joined(nn(two_parts(coarse), rows))
        return [out[:, i * GS : (i + 1) * GS] for i in range(rows.shape[1] // GS)]

    def inner_products(residual, image):
        cross = residual[0] * image[0]
        square = image[0] * image[0]
        for a in range(1, GA):
            cross = cross + residual[a] * image[a]
            square = square + image[a] * image[a]
        cross = jnp.sum(cross, axis=1, keepdims=True)
        square = jnp.sum(square, axis=1, keepdims=True)
        return jnp.where(lane == 0, cross, jnp.where(lane == 1, square, 0.0))

    def step_of(inner):
        return inner[:, 0:1] / (inner[:, 1:2] + EPSILON)

    nothing = jnp.zeros((R, GS), F32)
    coarse_r0 = coarse_of(r0)

    pl.semaphore_wait(barrier, NSEC - 1 + NAX - 1)

    send_halo(0, r0)
    send_x(0, coarse_r0, nothing)

    def turn(j, carry):
        k = (j * 27) % NSEC
        to = (s + k) % NSEC
        remote(
            inverse_hbm.at[:, pl.ds(pl.multiple_of(to * GS, GS), GS)],
            turned.at[k - 1], t_ssem, t_rsem, (to, q),
        )
        return carry

    lax.fori_loop(1, NSEC, turn, 0)

    halo_r0 = get_halo(0)
    solver_copy.wait()
    local_r0 = local_solve(r0, halo_r0)
    send_band(0, jnp.concatenate([local_r0[0], basis[0]], axis=0))
    coarse_sum, _ = get_x(0)
    own_copy.wait()
    wait_for(turned.at[pl.ds(0, NSEC - 1)], t_rsem)
    blocks = [turned[(s - p + NSEC - 1) % NSEC] for p in range(NSEC)]
    turned_matrix = jnp.concatenate(blocks, axis=0)

    send_y(0, coarse_sum, nothing)
    forward_band(0)
    pass_z(0)
    band_rows = get_band(0)
    band_basis = spread(band_rows[R:], z)
    y_own, y_band, _ = get_z(0)
    corr0 = [u + v for u, v in zip(local_r0, prolong(y_own, basis_z))]
    send_halo(1, corr0)
    band_corr0 = band_rows[:R] + prolong(y_band, band_basis)[0]
    halo = get_halo(1)
    image0 = apply_operator(corr0, halo, band_corr0)

    send_halo(2, image0)
    send_x(1, coarse_of(image0), inner_products(r0, image0))
    local_im = local_solve(image0, get_halo(2))
    send_band(1, jnp.concatenate([local_im[0], nothing], axis=0))
    coarse_sum, inner = get_x(1)
    send_y(1, coarse_sum, inner)
    forward_band(1)
    pass_z(1)
    band_rows = get_band(1)
    y_own, y_band, inner = get_z(1)
    diff = [u + v for u, v in zip(local_im, prolong(y_own, basis_z))]
    send_halo(3, diff)
    band_diff = band_rows[:R] + prolong(y_band, band_basis)[0]
    step0 = step_of(inner)
    corr1 = [u - step0 * v for u, v in zip(corr0, diff)]
    res1 = [u - step0 * v for u, v in zip(r0, image0)]
    image_diff = apply_operator(diff, get_halo(3), band_diff)
    image1 = [u - step0 * v for u, v in zip(image0, image_diff)]

    inner = inner_products(res1, image1)
    send_x(2, nothing, inner)
    _, inner = get_x(2)
    for t in range(NY):
        y_send[2, t, pl.ds(0, R)] = nothing
        y_send[2, t, pl.ds(R, R)] = nothing
        y_send[2, t, pl.ds(2 * R, R)] = inner
    for k in range(1, NY):
        remote(y_send.at[2, (y + k) % NY], y_recv.at[2, k - 1], y_ssem.at[2], y_rsem.at[2], y_peer(k))
    pass_z(2)
    _, _, inner = get_z(2)
    step1 = step_of(inner)
    for a in range(GA):
        sol_ref[:, a, :] = step0 * corr0[a] + step1 * corr1[a]
        res_ref[:, a, :] = res1[a] - step1 * image1[a]

    wait_for(turned.at[pl.ds(0, NSEC - 1)], t_ssem)
    for n in range(4):
        wait_for(h_recv.at[n], h_ssem.at[n])
    for n in range(3):
        wait_for(x_recv.at[n], x_ssem.at[n])
        wait_for(y_recv.at[n], y_ssem.at[n])
        wait_for(z_recv.at[n], z_ssem.at[n])
    for n in range(2):
        wait_for(b1s[n].at[pl.ds(1, NZ - 1)], b1_ssem.at[n])
        wait_for(b2s[n].at[pl.ds(1, NY - 1)], b2_ssem.at[n])


def on_device(
    right_side, mass_term, band_weight, band_shift, local_solver, coarse_inverse, coarse_basis
):
    vmem = pl.BlockSpec(memory_space=pltpu.VMEM)
    smem = pl.BlockSpec(memory_space=pltpu.SMEM)
    hbm = pl.BlockSpec(memory_space=pl.ANY)
    dma = pltpu.SemaphoreType.DMA
    out = jax.ShapeDtypeStruct(right_side.shape, F32)
    return pl.pallas_call(
        body,
        name="schwarz_steps",
        out_shape=(out, out),
        in_specs=[vmem, vmem, vmem, smem, vmem, hbm, hbm],
        out_specs=(vmem, vmem),
        scratch_shapes=[
            pltpu.VMEM((GA * GS, NEXT), BF16),
            pltpu.VMEM((NSEC, NV, GS), BF16),
            pltpu.VMEM((4, 3, R, GS), F32),
            pltpu.VMEM((4, 4, R, GS), F32),
            pltpu.VMEM((3, XROWS, GS), F32),
            pltpu.VMEM((3, NAX - 1, XROWS, GS), F32),
            pltpu.VMEM((3, NY, YROWS, GS), F32),
            pltpu.VMEM((3, NY - 1, YROWS, GS), F32),
            pltpu.VMEM((3, YROWS, GS), F32),
            pltpu.VMEM((3, NZ - 1, YROWS, GS), F32),
            pltpu.VMEM((NZ, 2 * R, GS), F32),
            pltpu.VMEM((NZ, 2 * R, GS), F32),
            pltpu.VMEM((NY, 2 * R, GS), F32),
            pltpu.VMEM((NY, 2 * R, GS), F32),
            pltpu.VMEM((NY, R, GS), F32),
            dma((2,)),
            dma,
            dma,
            dma((4,)),
            dma((4,)),
            dma((3,)),
            dma((3,)),
            dma((3,)),
            dma((3,)),
            dma((3,)),
            dma((3,)),
            dma((2,)),
            dma((2,)),
            dma((2,)),
            dma((2,)),
        ],
        compiler_params=pltpu.CompilerParams(
            collective_id=0, has_side_effects=True, vmem_limit_bytes=32 << 20
        ),
    )(right_side, mass_term, band_weight, band_shift, coarse_basis, local_solver, coarse_inverse)


def solution(mesh):
    placed = (
        P(None, "axial", "sector"),
        P("axial", "sector"),
        P("axial", "sector"),
        P(),
        P("axial", "sector", None),
        P(("sector", "axial"), None),
        P(None, "axial", "sector"),
    )
    return jax.shard_map(
        on_device,
        mesh=mesh,
        in_specs=placed,
        out_specs=(P(None, "axial", "sector"), P(None, "axial", "sector")),
        check_vma=False,
    )
```

time: 512 us -> 92.4 us (0.18)
  blocking collectives: 438 us -> 0 us
  Pallas kernels: 0 us -> 87 us
  starting transfers between devices: 45.2 us -> 0 us
  waiting for transfers between devices: 12.5 us -> 0 us
  matrix products: 8.72 us -> 0 us
    all_gather x4 -> x0, blocking collectives: 224 us -> none  [the longest x2 155 us: on_device(): lax.all_gather(jnp.einsum('lds,kds->lk', residual, basis_single_float32,...]
    psum x2 -> x0, blocking collectives: 214 us -> none  [on_device(): lax.psum((part_cross, part_square), ('sector', 'axial'))]
    pallas_call x0 -> x1, Pallas kernels: none -> 87 us  [on_device(): pl.pallas_call(body, name='schwarz_steps', out_shape=(out, out), in_specs...]
    ppermute x16 -> x0, starting transfers between devices: 45.2 us -> none  [the longest x8 34 us: with_halo(): after = lax.ppermute(first, axis, down)]
    ppermute x16 -> x0, waiting for transfers between devices: 12.5 us -> none  [the longest x8 12.2 us: with_halo(): before = lax.ppermute(last, axis, up)]
    dot_general x8 -> x0, matrix products: 8.72 us -> none  [the longest x2 6.99 us: on_device(): lax.dot_general(coarse_combined, inverse_rows, (((1,), (1,)), ((), ())),...]
  transfers between devices with their start and end apart: 16 -> 0, of which waited for: 4 -> 0; matrix products, arithmetic and copies ran while one was open for 2% -> 0% of each run, Pallas kernels for 0% -> 0%
where the time goes in v1:
time: 92.4 us; the launch traced here: 91.2 us
  Pallas kernels  87 us (94%)
  local copies, waits for them, and re-layouts  2.8 us (3%)
  between operations  1.37 us (1%)
    pallas_call x1, Pallas kernels, on_device(): pl.pallas_call(body, name='schwarz_steps', out_shape=(out, out), in_specs...  87 us
    unnamed x13, local copies, waits for them, and re-layouts  2.8 us

profile of v1, /device:TPU:1, one launch (start us, length us, event | category | flops | bytes accessed | tf_op | source)
XLA Modules:
  0.0 91.2 jit_solution(6450720505215615331)
XLA Ops:
  1.3 0.0 copy-start
  1.3 0.0 copy-start.1
  1.3 0.0 copy-start.2
  1.3 0.0 copy-start.3
  1.3 0.0 copy-start.4
  1.3 1.5 %copy.9.solver_hbm = bf16[1,512,780]{2,1,0:T(8,128)(2,1)S(1)} copy(bf16[1,512,780]{1,2,0:T(8,128)(2,1)} %param.11) | data formatting | bytes 1597440 | tf_op args[4]
  2.9 0.0 copy-done
  2.9 0.0 copy-done.1
  2.9 0.0 copy-done.2
  2.9 0.0 copy-done.3
  2.9 0.0 copy-done.4
  2.9 87.0 %schwarz_steps.1 = (f32[16,4,128]{2,1,0:T(4,128)S(1)}, f32[16,4,128]{2,1,0:T(4,128)S(1)}) custom-call(f32[16,4,128]{2,1,0:T(4,128)S(1)} %copy-done.1, f32[4,128]{1,0:T(4,128)S(1)} %copy-done.3, f32[1,128]{1,0:T(1,128)S(1)} %copy-done.4, s32[1]{0:T(128)S(6)} %copy.12.shift_ref, bf16[16,4,128]{2,1,0:T(4,128)(2,1)S(1)} %copy-done.2, ...), custom_call_target="tpu_custom_call" | custom-call | tf_op jit(solution)/shard_map/schwarz_steps/pallas_call | solution.py:348
  89.9 0.6 copy.13
  90.5 0.6 copy.14
Async XLA Ops:
  1.3 1.6 %copy-start = (bf16[16,8192]{1,0:T(8,128)(2,1)S(1)}, bf16[16,8192]{1,0:T(8,128)(2,1)}, u32[]{:S(2)}) copy-start(bf16[16,8192]{1,0:T(8,128)(2,1)} %inverse_hbm.1) | copy-start | bytes 786436
  1.3 1.6 %copy-start.1 = (f32[16,4,128]{2,1,0:T(4,128)S(1)}, f32[16,4,128]{2,1,0:T(4,128)}, u32[]{:S(2)}) copy-start(f32[16,4,128]{2,1,0:T(4,128)} %rhs_ref.1) | copy-start | bytes 98308
  1.3 1.6 %copy-start.2 = (bf16[16,4,128]{2,1,0:T(4,128)(2,1)S(1)}, bf16[16,4,128]{2,1,0:T(4,128)(2,1)}, u32[]{:S(2)}) copy-start(bf16[16,4,128]{2,1,0:T(4,128)(2,1)} %basis_ref.1) | copy-start | bytes 49156
  1.3 1.6 %copy-start.3 = (f32[4,128]{1,0:T(4,128)S(1)}, f32[4,128]{1,0:T(4,128)}, u32[]{:S(2)}) copy-start(f32[4,128]{1,0:T(4,128)} %mass_ref.1) | copy-start | bytes 6148
  1.3 1.6 %copy-start.4 = (f32[1,128]{1,0:T(1,128)S(1)}, f32[1,128]{1,0:T(1,128)}, u32[]{:S(2)}) copy-start(f32[1,128]{1,0:T(1,128)} %bw_ref.1) | copy-start | bytes 1540

commit v2 on v1

v2 whole, which is shorter than its diff:
```python
import jax
import jax.numpy as jnp
from jax import lax
from jax.experimental import pallas as pl
from jax.experimental.pallas import tpu as pltpu
from jax.sharding import PartitionSpec as P

EPSILON = 1e-06
MESH = pl.DeviceIdType.MESH
F32 = jnp.float32
BF16 = jnp.bfloat16

R = 16
GA = 4
GS = 128
NV = 16
NEXT = 780
NZ = 8
NY = 8
NSEC = NY * NZ
NAX = 8
XROWS = R + 8


def nt(a, b):
    return lax.dot_general(a, b, (((1,), (1,)), ((), ())), preferred_element_type=F32)


def nn(a, b):
    return lax.dot_general(a, b, (((1,), (0,)), ((), ())), preferred_element_type=F32)


def two_parts(x):
    high = x.astype(BF16)
    low = (x - high.astype(F32)).astype(BF16)
    return jnp.concatenate([high, low], axis=0)


def joined(x):
    half = x.shape[0] // 2
    return x[:half] + x[half:]


def body(
    rhs_ref, mass_ref, bw_ref, shift_ref, basis_ref, solver_hbm, inverse_hbm,
    sol_ref, res_ref,
    solver, inverse_y, h_send, h_recv, x_send, x_recv, z_tiles, y_send, y_recv,
    w_first, w_second, b1_first, b1_second, b2_first, b2_second, f_send, f_recv,
    local_sems, m_ssem, m_rsem, h_ssem, h_rsem, x_ssem, x_rsem, z_ssem, z_rsem,
    y_ssem, y_rsem, w_ssem, w_rsem, b1_ssem, b1_rsem, b2_ssem, b2_rsem, f_ssem, f_rsem,
):
    ws = (w_first, w_second)
    b1s = (b1_first, b1_second)
    b2s = (b2_first, b2_second)
    s = lax.axis_index("sector")
    q = lax.axis_index("axial")
    y = s // NZ
    z = s % NZ

    def x_peer(k):
        return (s, (q + k) % NAX)

    def y_peer(k):
        return (((y + k) % NY) * NZ + z, q)

    def z_peer(k):
        return (y * NZ + (z + k) % NZ, q)

    def s_peer(k):
        return ((s + k) % NSEC, q)

    def wait_for(ref, sem):
        pltpu.make_async_copy(ref, ref, sem).wait()

    def remote(src, dst, ssem, rsem, device):
        pltpu.make_async_remote_copy(
            src_ref=src, dst_ref=dst, send_sem=ssem, recv_sem=rsem,
            device_id=device, device_id_type=MESH,
        ).start()

    barrier = pltpu.get_barrier_semaphore()
    for k in range(1, 8):
        for peer in (y_peer(k), z_peer(k), x_peer(k)):
            pl.semaphore_signal(barrier, inc=1, device_id=peer, device_id_type=MESH)
    for k in (1, NSEC - 1):
        pl.semaphore_signal(barrier, inc=1, device_id=s_peer(k), device_id_type=MESH)

    solver_copy = pltpu.make_async_copy(solver_hbm.at[0], solver, local_sems.at[0])
    solver_copy.start()

    def inverse_for(to):
        return inverse_hbm.at[:, pl.ds(pl.multiple_of(to * NZ * GS, NZ * GS), NZ * GS)]

    own_copy = pltpu.make_async_copy(inverse_for(y), inverse_y.at[y], local_sems.at[1])
    own_copy.start()

    lane = lax.broadcasted_iota(jnp.int32, (R, GS), 1)
    lane8 = lax.broadcasted_iota(jnp.int32, (8, GS), 1)
    rows128 = lax.broadcasted_iota(jnp.int32, (8 * NV, GS), 0) // NV
    rhs = rhs_ref[...]
    r0 = [rhs[:, a, :] for a in range(GA)]
    basis_all = basis_ref[...].astype(F32)
    basis = [basis_all[:, a, :] for a in range(GA)]
    mass = [mass_ref[a : a + 1, :] + 4.0 for a in range(GA)]
    weight = bw_ref[...]
    shift = shift_ref[0]
    shift_z = shift % NZ
    shift_y = (shift // NZ + jnp.where(z < shift_z, 1, 0)) % NY

    def spread(tile, at):
        return jnp.where(rows128 == at, jnp.concatenate([tile] * 8, axis=0), 0.0).astype(BF16)

    basis_q = jnp.concatenate([spread(t, q) for t in basis], axis=1)
    basis_y = jnp.concatenate([spread(t, y) for t in basis], axis=1)

    def coarse_of(field):
        return joined(nt(two_parts(jnp.concatenate(field, axis=1)), basis_q))

    def edges(field):
        tile = jnp.zeros((R, GS), F32)
        for a in range(GA):
            at = 2 * (a + 1)
            moved = pltpu.roll(field[a], at + 1, 1)
            tile = jnp.where((lane == at) | (lane == at + 1), moved, tile)
        return tile

    def send_halo(n, field):
        h_send[n, 0] = edges(field)
        h_send[n, 1] = field[0]
        h_send[n, 2] = field[GA - 1]
        remote(h_send.at[n, 0], h_recv.at[n, 0], h_ssem.at[n], h_rsem.at[n], s_peer(1))
        remote(h_send.at[n, 0], h_recv.at[n, 1], h_ssem.at[n], h_rsem.at[n], s_peer(NSEC - 1))
        remote(h_send.at[n, 2], h_recv.at[n, 2], h_ssem.at[n], h_rsem.at[n], x_peer(1))
        remote(h_send.at[n, 1], h_recv.at[n, 3], h_ssem.at[n], h_rsem.at[n], x_peer(NAX - 1))

    def get_halo(n):
        wait_for(h_recv.at[n], h_rsem.at[n])
        above = jnp.where(q == 0, 0.0, h_recv[n, 2])
        below = jnp.where(q == NAX - 1, 0.0, h_recv[n, 3])
        return h_recv[n, 0], h_recv[n, 1], above, below

    def local_solve(field, halo):
        left, right, above, below = halo
        stack = [above] + field + [below]
        moved = [pltpu.roll(stack[j], 2 * j + 1, 1) for j in range(GA + 2)]
        zero = jnp.zeros((R, GS), F32)
        parts = []
        for t in range(GA + 3):
            here = moved[t] if t < GA + 2 else zero
            before = moved[t - 1] if t > 0 else zero
            tile = jnp.where(lane == 2 * t - 1, right, before)
            tile = jnp.where(lane == 2 * t, left, tile)
            parts.append(jnp.where(lane > 2 * t, here, tile))
        window = jnp.concatenate(parts, axis=1)
        out = joined(nn(two_parts(window)[:, :NEXT], solver[...]))
        return [out[:, a * GS : (a + 1) * GS] for a in range(GA)]

    def apply_operator(field, halo, band):
        left, right, above, below = halo
        stack = [above] + field + [below]
        image = []
        for a in range(GA):
            u = field[a]
            before = jnp.where(lane == 0, pltpu.roll(left, GS - 2 * (a + 1), 1), pltpu.roll(u, 1, 1))
            after = jnp.where(
                lane == GS - 1, pltpu.roll(right, GS - 1 - (2 * a + 3), 1), pltpu.roll(u, GS - 1, 1)
            )
            value = mass[a] * u - ((stack[a + 2] + stack[a]) + before + after)
            if a == 0:
                value = value + weight * (u - band)
            image.append(value)
        return image

    def send_band(n, rows):
        b1s[n][0] = rows
        for k in range(1, NZ):
            remote(b1s[n].at[0], b1s[n].at[k], b1_ssem.at[n], b1_rsem.at[n], z_peer(k))

    def forward_band(n):
        wait_for(b1s[n].at[pl.ds(1, NZ - 1)], b1_rsem.at[n])
        b2s[n][0] = b1s[n][shift_z]
        for k in range(1, NY):
            remote(b2s[n].at[0], b2s[n].at[k], b2_ssem.at[n], b2_rsem.at[n], y_peer(k))

    def get_band(n):
        wait_for(b2s[n].at[pl.ds(1, NY - 1)], b2_rsem.at[n])
        return b2s[n][shift_y]

    def rows_of(n):
        return pl.ds(0, R if n == 0 else XROWS)

    def send_x(n, coarse, inner):
        x_send[n, pl.ds(0, R)] = coarse
        if inner is not None:
            x_send[n, pl.ds(R, 8)] = inner
        for k in range(1, NAX):
            remote(
                x_send.at[n, rows_of(n)], x_recv.at[n, k - 1, rows_of(n)],
                x_ssem.at[n], x_rsem.at[n], x_peer(k),
            )

    def pass_z(n):
        wait_for(x_recv.at[n, :, rows_of(n)], x_rsem.at[n])
        total = x_send[n, rows_of(n)]
        for k in range(NAX - 1):
            total = total + x_recv[n, k, rows_of(n)]
        z_tiles[n, z, rows_of(n)] = total
        for k in range(1, NZ):
            remote(
                z_tiles.at[n, z, rows_of(n)], z_tiles.at[n, z, rows_of(n)],
                z_ssem.at[n], z_rsem.at[n], z_peer(k),
            )

    def pass_y(n):
        wait_for(z_tiles.at[n, pl.ds(0, NZ - 1), rows_of(n)], z_rsem.at[n])
        gathered = jnp.concatenate([z_tiles[n, t, pl.ds(0, R)] for t in range(NZ)], axis=1)
        if n == 0:
            own_copy.wait()
            wait_for(inverse_y.at[pl.ds(0, NY - 1)], m_rsem)
        matrix = jnp.concatenate([inverse_y[t] for t in range(NY)], axis=0)
        y_send[n, pl.ds(0, R)] = joined(nt(two_parts(gathered), matrix))
        if n > 0:
            inner = z_tiles[n, 0, pl.ds(R, 8)]
            for t in range(1, NZ):
                inner = inner + z_tiles[n, t, pl.ds(R, 8)]
            y_send[n, pl.ds(R, 8)] = inner
        for k in range(1, NY):
            remote(
                y_send.at[n, rows_of(n)], y_recv.at[n, k - 1, rows_of(n)],
                y_ssem.at[n], y_rsem.at[n], y_peer(k),
            )

    def get_y(n):
        wait_for(y_recv.at[n, :, rows_of(n)], y_rsem.at[n])
        total = y_send[n, rows_of(n)]
        for k in range(NY - 1):
            total = total + y_recv[n, k, rows_of(n)]
        return total[:R], total[R:]

    def send_coarse(n, tile):
        ws[n][0] = tile
        for k in range(1, NZ):
            remote(ws[n].at[0], ws[n].at[k], w_ssem.at[n], w_rsem.at[n], z_peer(k))

    def get_coarse(n):
        wait_for(ws[n].at[pl.ds(1, NZ - 1)], w_rsem.at[n])
        return ws[n][shift_z]

    def prolong(coarse, rows):
        out = joined(nn(two_parts(coarse), rows))
        return [out[:, i * GS : (i + 1) * GS] for i in range(rows.shape[1] // GS)]

    def inner_products(residual, image):
        cross = residual[0] * image[0]
        square = image[0] * image[0]
        for a in range(1, GA):
            cross = cross + residual[a] * image[a]
            square = square + image[a] * image[a]
        cross = jnp.sum(cross, axis=1, keepdims=True)
        square = jnp.sum(square, axis=1, keepdims=True)
        tile = jnp.zeros((8, GS), F32)
        for i, column in enumerate((cross[:8], square[:8], cross[8:], square[8:])):
            tile = jnp.where(lane8 == i, column, tile)
        return tile

    def step_of(inner):
        cross = jnp.concatenate([inner[:, 0:1], inner[:, 2:3]], axis=0)
        square = jnp.concatenate([inner[:, 1:2], inner[:, 3:4]], axis=0)
        return cross / (square + EPSILON)

    coarse_r0 = coarse_of(r0)

    pl.semaphore_wait(barrier, 7 + 7 + 7 + 2)

    send_x(0, coarse_r0, None)
    send_halo(0, r0)
    for k in range(1, NY):
        remote(inverse_for((y + k) % NY), inverse_y.at[y], m_ssem, m_rsem, y_peer(k))
    pass_z(0)
    halo_r0 = get_halo(0)
    solver_copy.wait()
    local_r0 = local_solve(r0, halo_r0)
    send_band(0, jnp.concatenate([local_r0[0], basis[0]], axis=0))
    pass_y(0)
    forward_band(0)
    coarse, _ = get_y(0)
    send_coarse(0, coarse)
    corr0 = [u + v for u, v in zip(local_r0, prolong(coarse, basis_y))]
    send_halo(1, corr0)
    band_rows = get_band(0)
    band_basis = spread(band_rows[R:], (y + NY - shift_y) % NY)
    band_corr0 = band_rows[:R] + prolong(get_coarse(0), band_basis)[0]
    image0 = apply_operator(corr0, get_halo(1), band_corr0)

    send_x(1, coarse_of(image0), inner_products(r0, image0))
    send_halo(2, image0)
    pass_z(1)
    local_im = local_solve(image0, get_halo(2))
    send_band(1, local_im[0])
    pass_y(1)
    forward_band(1)
    coarse, inner = get_y(1)
    send_coarse(1, coarse)
    diff = [u + v for u, v in zip(local_im, prolong(coarse, basis_y))]
    send_halo(3, diff)
    step0 = step_of(inner)
    corr1 = [u - step0 * v for u, v in zip(corr0, diff)]
    res1 = [u - step0 * v for u, v in zip(r0, image0)]
    band_row = get_band(1)
    band_diff = band_row + prolong(get_coarse(1), band_basis)[0]
    image_diff = apply_operator(diff, get_halo(3), band_diff)
    image1 = [u - step0 * v for u, v in zip(image0, image_diff)]

    inner = inner_products(res1, image1)
    for i, peer in enumerate((x_peer, y_peer, z_peer)):
        f_send[i] = inner
        for k in range(1, 8):
            remote(f_send.at[i], f_recv.at[i, k - 1], f_ssem.at[i], f_rsem.at[i], peer(k))
        wait_for(f_recv.at[i], f_rsem.at[i])
        for k in range(7):
            inner = inner + f_recv[i, k]
    step1 = step_of(inner)
    for a in range(GA):
        sol_ref[:, a, :] = step0 * corr0[a] + step1 * corr1[a]
        res_ref[:, a, :] = res1[a] - step1 * image1[a]

    wait_for(inverse_y.at[pl.ds(0, NY - 1)], m_ssem)
    for n in range(4):
        wait_for(h_recv.at[n], h_ssem.at[n])
    for n in range(2):
        wait_for(x_recv.at[n, :, rows_of(n)], x_ssem.at[n])
        wait_for(z_tiles.at[n, pl.ds(0, NZ - 1), rows_of(n)], z_ssem.at[n])
        wait_for(y_recv.at[n, :, rows_of(n)], y_ssem.at[n])
        wait_for(ws[n].at[pl.ds(1, NZ - 1)], w_ssem.at[n])
        wait_for(b1s[n].at[pl.ds(1, NZ - 1)], b1_ssem.at[n])
        wait_for(b2s[n].at[pl.ds(1, NY - 1)], b2_ssem.at[n])
    for i in range(3):
        wait_for(f_recv.at[i], f_ssem.at[i])


def on_device(
    right_side, mass_term, band_weight, band_shift, local_solver, coarse_inverse, coarse_basis
):
    vmem = pl.BlockSpec(memory_space=pltpu.VMEM)
    smem = pl.BlockSpec(memory_space=pltpu.SMEM)
    hbm = pl.BlockSpec(memory_space=pltpu.HBM)
    dma = pltpu.SemaphoreType.DMA
    out = jax.ShapeDtypeStruct(right_side.shape, F32)

    def tiles(*shape):
        return pltpu.VMEM(shape + (GS,), F32)

    return pl.pallas_call(
        body,
        name="schwarz_steps",
        out_shape=(out, out),
        in_specs=[vmem, vmem, vmem, smem, vmem, hbm, hbm],
        out_specs=(vmem, vmem),
        scratch_shapes=[
            pltpu.VMEM((NEXT, GA * GS), BF16),
            pltpu.VMEM((NY, NV, NZ * GS), BF16),
            tiles(4, 3, R),
            tiles(4, 4, R),
            tiles(2, XROWS),
            tiles(2, NAX - 1, XROWS),
            tiles(2, NZ, XROWS),
            tiles(2, XROWS),
            tiles(2, NY - 1, XROWS),
            tiles(NZ, R),
            tiles(NZ, R),
            tiles(NZ, 2 * R),
            tiles(NZ, R),
            tiles(NY, 2 * R),
            tiles(NY, R),
            tiles(3, 8),
            tiles(3, 7, 8),
            dma((2,)),
            dma,
            dma,
            dma((4,)),
            dma((4,)),
        ]
        + [dma((2,))] * 12
        + [dma((3,))] * 2,
        compiler_params=pltpu.CompilerParams(
            collective_id=0, has_side_effects=True, vmem_limit_bytes=32 << 20
        ),
    )(
        right_side, mass_term, band_weight, band_shift, coarse_basis,
        jnp.swapaxes(local_solver, 1, 2), coarse_inverse,
    )


def solution(mesh):
    placed = (
        P(None, "axial", "sector"),
        P("axial", "sector"),
        P("axial", "sector"),
        P(),
        P("axial", "sector", None),
        P(("sector", "axial"), None),
        P(None, "axial", "sector"),
    )
    return jax.shard_map(
        on_device,
        mesh=mesh,
        in_specs=placed,
        out_specs=(P(None, "axial", "sector"), P(None, "axial", "sector")),
        check_vma=False,
    )
```

time: 92.4 us -> 75.6 us (0.82)
  Pallas kernels: 87 us -> 68.2 us
  local copies, waits for them, and re-layouts: 2.8 us -> 5.44 us
    pallas_call x1, Pallas kernels: 87 us -> 68.2 us  [on_device(): pl.pallas_call(body, name='schwarz_steps', out_shape=(out, out), in_specs...]
    unnamed x13 -> x14, local copies, waits for them, and re-layouts: 2.8 us -> 5.44 us
where the time goes in v2:
time: 75.6 us; the launch traced here: 75 us
  Pallas kernels  68.2 us (90%)
  local copies, waits for them, and re-layouts  5.44 us (7%)
  between operations  1.32 us (2%)
    pallas_call x1, Pallas kernels, on_device(): pl.pallas_call(body, name='schwarz_steps', out_shape=(out, out), in_specs...  68.2 us
    unnamed x14, local copies, waits for them, and re-layouts  5.44 us

profile of v2, /device:TPU:1, one launch (start us, length us, event | category | flops | bytes accessed | tf_op | source)
XLA Modules:
  0.0 75.0 jit_solution(7357213189374600051)
XLA Ops:
  0.6 0.0 copy-start.4
  1.3 0.0 copy-start.5
  1.3 0.0 copy-done.4
  1.3 0.6 copy-done.5
  2.0 0.0 copy-start
  2.0 1.1 %copy-done = bf16[1,512,780]{1,2,0:T(8,128)(2,1)S(1)} copy-done((bf16[1,512,780]{1,2,0:T(8,128)(2,1)S(1)}, bf16[1,512,780]{1,2,0:T(8,128)(2,1)}, u32[]{:S(2)}) %copy-start) | copy-done | bytes 798744
  3.1 0.0 copy-start.1
  3.1 0.9 %copy-done.1 = bf16[16,8192]{1,0:T(8,128)(2,1)S(1)} copy-done((bf16[16,8192]{1,0:T(8,128)(2,1)S(1)}, bf16[16,8192]{1,0:T(8,128)(2,1)}, u32[]{:S(2)}) %copy-start.1) | copy-done | bytes 262168
  4.0 0.0 copy-start.2
  4.0 0.8 %copy-done.2 = f32[16,4,128]{2,1,0:T(4,128)S(1)} copy-done((f32[16,4,128]{2,1,0:T(4,128)S(1)}, f32[16,4,128]{2,1,0:T(4,128)}, u32[]{:S(2)}) %copy-start.2) | copy-done | bytes 32792
  4.8 0.0 copy-start.3
  4.8 0.7 copy-done.3
  5.5 68.2 %schwarz_steps.1 = (f32[16,4,128]{2,1,0:T(4,128)S(1)}, f32[16,4,128]{2,1,0:T(4,128)S(1)}) custom-call(f32[16,4,128]{2,1,0:T(4,128)S(1)} %copy-done.2, f32[4,128]{1,0:T(4,128)S(1)} %copy-done.4, f32[1,128]{1,0:T(1,128)S(1)} %copy-done.5, s32[1]{0:T(128)S(6)} %copy.11.shift_ref, bf16[16,4,128]{2,1,0:T(4,128)(2,1)S(1)} %copy-done.3, ...), custom_call_target="tpu_custom_call" | custom-call | tf_op jit(solution)/shard_map/schwarz_steps/pallas_call | solution.py:353
  73.7 0.6 copy.12
  74.3 0.6 copy.13
Async XLA Ops:
  0.6 0.7 copy-start.4
  1.3 0.7 copy-start.5
  2.0 1.1 %copy-start = (bf16[1,512,780]{1,2,0:T(8,128)(2,1)S(1)}, bf16[1,512,780]{1,2,0:T(8,128)(2,1)}, u32[]{:S(2)}) copy-start(bf16[1,512,780]{1,2,0:T(8,128)(2,1)} %param.11) | copy-start | bytes 2396164
  3.1 0.9 %copy-start.1 = (bf16[16,8192]{1,0:T(8,128)(2,1)S(1)}, bf16[16,8192]{1,0:T(8,128)(2,1)}, u32[]{:S(2)}) copy-start(bf16[16,8192]{1,0:T(8,128)(2,1)} %inverse_hbm.1) | copy-start | bytes 786436
  4.0 0.8 %copy-start.2 = (f32[16,4,128]{2,1,0:T(4,128)S(1)}, f32[16,4,128]{2,1,0:T(4,128)}, u32[]{:S(2)}) copy-start(f32[16,4,128]{2,1,0:T(4,128)} %rhs_ref.1) | copy-start | bytes 98308
  4.8 0.7 copy-start.3

commit v3 on v2

--- a/solution.py
+++ b/solution.py
@@ -20,6 +20,7 @@
 NSEC = NY * NZ
 NAX = 8
 XROWS = R + 8
+FAR_FIRST = (4, 3, 5, 2, 6, 1, 7)
 
 
 def nt(a, b):
@@ -42,11 +43,12 @@
 
 
 def body(
-    rhs_ref, mass_ref, bw_ref, shift_ref, basis_ref, solver_hbm, inverse_hbm,
+    rhs_hbm, mass_hbm, bw_hbm, shift_ref, basis_hbm, solver_hbm, inverse_hbm,
     sol_ref, res_ref,
+    rhs_ref, mass_ref, bw_ref, basis_ref,
     solver, inverse_y, h_send, h_recv, x_send, x_recv, z_tiles, y_send, y_recv,
-    w_first, w_second, b1_first, b1_second, b2_first, b2_second, f_send, f_recv,
-    local_sems, m_ssem, m_rsem, h_ssem, h_rsem, x_ssem, x_rsem, z_ssem, z_rsem,
+    w_first, w_second, b1_first, b1_second, b2_first, b2_second, basis_moved, f_send, f_recv,
+    local_sems, c_ssem, c_rsem, m_ssem, m_rsem, h_ssem, h_rsem, x_ssem, x_rsem, z_ssem, z_rsem,
     y_ssem, y_rsem, w_ssem, w_rsem, b1_ssem, b1_rsem, b2_ssem, b2_rsem, f_ssem, f_rsem,
 ):
     ws = (w_first, w_second)
@@ -78,25 +80,36 @@
             device_id=device, device_id_type=MESH,
         ).start()
 
+    loads = [
+        pltpu.make_async_copy(src, dst, local_sems.at[i])
+        for i, (src, dst) in enumerate(
+            ((rhs_hbm, rhs_ref), (basis_hbm, basis_ref), (mass_hbm, mass_ref), (bw_hbm, bw_ref))
+        )
+    ]
+    for load in loads:
+        load.start()
+
     barrier = pltpu.get_barrier_semaphore()
-    for k in range(1, 8):
+    for k in FAR_FIRST:
         for peer in (y_peer(k), z_peer(k), x_peer(k)):
             pl.semaphore_signal(barrier, inc=1, device_id=peer, device_id_type=MESH)
     for k in (1, NSEC - 1):
         pl.semaphore_signal(barrier, inc=1, device_id=s_peer(k), device_id_type=MESH)
 
-    solver_copy = pltpu.make_async_copy(solver_hbm.at[0], solver, local_sems.at[0])
+    solver_copy = pltpu.make_async_copy(solver_hbm.at[0], solver, local_sems.at[4])
     solver_copy.start()
 
     def inverse_for(to):
         return inverse_hbm.at[:, pl.ds(pl.multiple_of(to * NZ * GS, NZ * GS), NZ * GS)]
 
-    own_copy = pltpu.make_async_copy(inverse_for(y), inverse_y.at[y], local_sems.at[1])
+    own_copy = pltpu.make_async_copy(inverse_for(y), inverse_y.at[y], local_sems.at[5])
     own_copy.start()
 
     lane = lax.broadcasted_iota(jnp.int32, (R, GS), 1)
     lane8 = lax.broadcasted_iota(jnp.int32, (8, GS), 1)
     rows128 = lax.broadcasted_iota(jnp.int32, (8 * NV, GS), 0) // NV
+    for load in loads:
+        load.wait()
     rhs = rhs_ref[...]
     r0 = [rhs[:, a, :] for a in range(GA)]
     basis_all = basis_ref[...].astype(F32)
@@ -105,7 +118,8 @@
     weight = bw_ref[...]
     shift = shift_ref[0]
     shift_z = shift % NZ
-    shift_y = (shift // NZ + jnp.where(z < shift_z, 1, 0)) % NY
+    up = (shift // NZ + jnp.where(z < shift_z, 1, 0)) % NY
+    up_there = (shift // NZ + jnp.where(z + shift_z >= NZ, 1, 0)) % NY
 
     def spread(tile, at):
         return jnp.where(rows128 == at, jnp.concatenate([tile] * 8, axis=0), 0.0).astype(BF16)
@@ -173,18 +187,21 @@
 
     def send_band(n, rows):
         b1s[n][0] = rows
-        for k in range(1, NZ):
-            remote(b1s[n].at[0], b1s[n].at[k], b1_ssem.at[n], b1_rsem.at[n], z_peer(k))
+        for k in FAR_FIRST:
+            remote(b1s[n].at[0], b1s[n].at[k], b1_ssem.at[n], b1_rsem.at[n], y_peer(k))
 
     def forward_band(n):
-        wait_for(b1s[n].at[pl.ds(1, NZ - 1)], b1_rsem.at[n])
-        b2s[n][0] = b1s[n][shift_z]
-        for k in range(1, NY):
-            remote(b2s[n].at[0], b2s[n].at[k], b2_ssem.at[n], b2_rsem.at[n], y_peer(k))
+        wait_for(b1s[n].at[pl.ds(1, NY - 1)], b1_rsem.at[n])
+        b2s[n][0, pl.ds(0, R)] = b1s[n][up_there]
+        if n == 0:
+            wait_for(basis_moved.at[pl.ds(1, NY - 1)], c_rsem)
+            b2s[n][0, pl.ds(R, R)] = basis_moved[up_there].astype(F32)
+        for k in FAR_FIRST:
+            remote(b2s[n].at[0], b2s[n].at[k], b2_ssem.at[n], b2_rsem.at[n], z_peer(k))
 
     def get_band(n):
-        wait_for(b2s[n].at[pl.ds(1, NY - 1)], b2_rsem.at[n])
-        return b2s[n][shift_y]
+        wait_for(b2s[n].at[pl.ds(1, NZ - 1)], b2_rsem.at[n])
+        return b2s[n][shift_z]
 
     def rows_of(n):
         return pl.ds(0, R if n == 0 else XROWS)
@@ -193,7 +210,7 @@
         x_send[n, pl.ds(0, R)] = coarse
         if inner is not None:
             x_send[n, pl.ds(R, 8)] = inner
-        for k in range(1, NAX):
+        for k in FAR_FIRST:
             remote(
                 x_send.at[n, rows_of(n)], x_recv.at[n, k - 1, rows_of(n)],
                 x_ssem.at[n], x_rsem.at[n], x_peer(k),
@@ -205,7 +222,7 @@
         for k in range(NAX - 1):
             total = total + x_recv[n, k, rows_of(n)]
         z_tiles[n, z, rows_of(n)] = total
-        for k in range(1, NZ):
+        for k in FAR_FIRST:
             remote(
                 z_tiles.at[n, z, rows_of(n)], z_tiles.at[n, z, rows_of(n)],
                 z_ssem.at[n], z_rsem.at[n], z_peer(k),
@@ -224,7 +241,7 @@
             for t in range(1, NZ):
                 inner = inner + z_tiles[n, t, pl.ds(R, 8)]
             y_send[n, pl.ds(R, 8)] = inner
-        for k in range(1, NY):
+        for k in FAR_FIRST:
             remote(
                 y_send.at[n, rows_of(n)], y_recv.at[n, k - 1, rows_of(n)],
                 y_ssem.at[n], y_rsem.at[n], y_peer(k),
@@ -239,7 +256,7 @@
 
     def send_coarse(n, tile):
         ws[n][0] = tile
-        for k in range(1, NZ):
+        for k in FAR_FIRST:
             remote(ws[n].at[0], ws[n].at[k], w_ssem.at[n], w_rsem.at[n], z_peer(k))
 
     def get_coarse(n):
@@ -273,14 +290,17 @@
     pl.semaphore_wait(barrier, 7 + 7 + 7 + 2)
 
     send_x(0, coarse_r0, None)
+    basis_moved[0] = basis[0].astype(BF16)
+    for k in FAR_FIRST:
+        remote(basis_moved.at[0], basis_moved.at[k], c_ssem, c_rsem, y_peer(k))
     send_halo(0, r0)
-    for k in range(1, NY):
+    for k in FAR_FIRST:
         remote(inverse_for((y + k) % NY), inverse_y.at[y], m_ssem, m_rsem, y_peer(k))
     pass_z(0)
     halo_r0 = get_halo(0)
     solver_copy.wait()
     local_r0 = local_solve(r0, halo_r0)
-    send_band(0, jnp.concatenate([local_r0[0], basis[0]], axis=0))
+    send_band(0, local_r0[0])
     pass_y(0)
     forward_band(0)
     coarse, _ = get_y(0)
@@ -288,7 +308,7 @@
     corr0 = [u + v for u, v in zip(local_r0, prolong(coarse, basis_y))]
     send_halo(1, corr0)
     band_rows = get_band(0)
-    band_basis = spread(band_rows[R:], (y + NY - shift_y) % NY)
+    band_basis = spread(band_rows[R:], (y + NY - up) % NY)
     band_corr0 = band_rows[:R] + prolong(get_coarse(0), band_basis)[0]
     image0 = apply_operator(corr0, get_halo(1), band_corr0)
 
@@ -314,7 +334,7 @@
     inner = inner_products(res1, image1)
     for i, peer in enumerate((x_peer, y_peer, z_peer)):
         f_send[i] = inner
-        for k in range(1, 8):
+        for k in FAR_FIRST:
             remote(f_send.at[i], f_recv.at[i, k - 1], f_ssem.at[i], f_rsem.at[i], peer(k))
         wait_for(f_recv.at[i], f_rsem.at[i])
         for k in range(7):
@@ -325,6 +345,7 @@
         res_ref[:, a, :] = res1[a] - step1 * image1[a]
 
     wait_for(inverse_y.at[pl.ds(0, NY - 1)], m_ssem)
+    wait_for(basis_moved.at[pl.ds(1, NY - 1)], c_ssem)
     for n in range(4):
         wait_for(h_recv.at[n], h_ssem.at[n])
     for n in range(2):
@@ -332,8 +353,8 @@
         wait_for(z_tiles.at[n, pl.ds(0, NZ - 1), rows_of(n)], z_ssem.at[n])
         wait_for(y_recv.at[n, :, rows_of(n)], y_ssem.at[n])
         wait_for(ws[n].at[pl.ds(1, NZ - 1)], w_ssem.at[n])
-        wait_for(b1s[n].at[pl.ds(1, NZ - 1)], b1_ssem.at[n])
-        wait_for(b2s[n].at[pl.ds(1, NY - 1)], b2_ssem.at[n])
+        wait_for(b1s[n].at[pl.ds(1, NY - 1)], b1_ssem.at[n])
+        wait_for(b2s[n].at[pl.ds(1, NZ - 1)], b2_ssem.at[n])
     for i in range(3):
         wait_for(f_recv.at[i], f_ssem.at[i])
 
@@ -354,9 +375,13 @@
         body,
         name="schwarz_steps",
         out_shape=(out, out),
-        in_specs=[vmem, vmem, vmem, smem, vmem, hbm, hbm],
+        in_specs=[hbm, hbm, hbm, smem, hbm, hbm, hbm],
         out_specs=(vmem, vmem),
         scratch_shapes=[
+            pltpu.VMEM(right_side.shape, F32),
+            pltpu.VMEM(mass_term.shape, F32),
+            pltpu.VMEM(band_weight.shape, F32),
+            pltpu.VMEM(coarse_basis.shape, BF16),
             pltpu.VMEM((NEXT, GA * GS), BF16),
             pltpu.VMEM((NY, NV, NZ * GS), BF16),
             tiles(4, 3, R),
@@ -368,13 +393,16 @@
             tiles(2, NY - 1, XROWS),
             tiles(NZ, R),
             tiles(NZ, R),
+            tiles(NY, R),
+            tiles(NY, R),
             tiles(NZ, 2 * R),
             tiles(NZ, R),
-            tiles(NY, 2 * R),
-            tiles(NY, R),
+            pltpu.VMEM((NY, NV, GS), BF16),
             tiles(3, 8),
             tiles(3, 7, 8),
-            dma((2,)),
+            dma((6,)),
+            dma,
+            dma,
             dma,
             dma,
             dma((4,)),
@@ -383,7 +411,7 @@
         + [dma((2,))] * 12
         + [dma((3,))] * 2,
         compiler_params=pltpu.CompilerParams(
-            collective_id=0, has_side_effects=True, vmem_limit_bytes=32 << 20
+            collective_id=0, has_side_effects=True, vmem_limit_bytes=60 << 20
         ),
     )(
         right_side, mass_term, band_weight, band_shift, coarse_basis,

time: 75.6 us -> 68.4 us (0.905)
  local copies, waits for them, and re-layouts: 5.44 us -> 2 us
  Pallas kernels: 68.2 us -> 64.8 us
    unnamed x14 -> x4, local copies, waits for them, and re-layouts: 5.44 us -> 2 us
    pallas_call x1, Pallas kernels: 68.2 us -> 64.8 us  [on_device(): pl.pallas_call(body, name='schwarz_steps', out_shape=(out, out), in_specs...]
where the time goes in v3:
time: 68.4 us; the launch traced here: 68.1 us
  Pallas kernels  64.8 us (95%)
  local copies, waits for them, and re-layouts  2 us (3%)
  between operations  1.29 us (2%)
    pallas_call x1, Pallas kernels, on_device(): pl.pallas_call(body, name='schwarz_steps', out_shape=(out, out), in_specs...  64.8 us
    unnamed x4, local copies, waits for them, and re-layouts  2 us

profile of v3, /device:TPU:1, one launch (start us, length us, event | category | flops | bytes accessed | tf_op | source)
XLA Modules:
  0.0 68.1 jit_solution(16209987426531745320)
XLA Ops:
  1.3 64.8 %schwarz_steps.1 = (f32[16,4,128]{2,1,0:T(4,128)}, f32[16,4,128]{2,1,0:T(4,128)}) custom-call(f32[16,4,128]{2,1,0:T(4,128)} %rhs_hbm.1, f32[4,128]{1,0:T(4,128)} %mass_hbm.1, f32[1,128]{1,0:T(1,128)} %bw_hbm.1, s32[1]{0:T(128)S(6)} %copy.11.shift_ref, bf16[16,4,128]{2,1,0:T(4,128)(2,1)} %basis_hbm.1, bf16[1,780,512]{2,1,0:T(8,128)(2,1)} %bitcast.1, ...), custom_call_target="tpu_custom_call" | custom-call | tf_op jit(solution)/shard_map/schwarz_steps/pallas_call | solution.py:374
  66.1 0.0 copy-start
  66.1 1.4 %copy.12 = f32[16,4,128]{2,1,0:T(4,128)} copy(f32[16,4,128]{2,1,0:T(4,128)} %get-tuple-element.4) | data formatting | bytes 65536
  67.5 0.0 copy-done
  67.5 0.6 copy.13
Async XLA Ops:
  66.1 1.4 %copy-start = (f32[16,4,128]{2,1,0:T(4,128)S(1)}, f32[16,4,128]{2,1,0:T(4,128)}, u32[]{:S(2)}) copy-start(f32[16,4,128]{2,1,0:T(4,128)} %get-tuple-element.5) | copy-start | bytes 98308

commit v4 on v3

--- a/solution.py
+++ b/solution.py
@@ -19,7 +19,6 @@
 NY = 8
 NSEC = NY * NZ
 NAX = 8
-XROWS = R + 8
 FAR_FIRST = (4, 3, 5, 2, 6, 1, 7)
 
 
@@ -44,12 +43,12 @@
 
 def body(
     rhs_hbm, mass_hbm, bw_hbm, shift_ref, basis_hbm, solver_hbm, inverse_hbm,
-    sol_ref, res_ref,
+    out_ref,
     rhs_ref, mass_ref, bw_ref, basis_ref,
     solver, inverse_y, h_send, h_recv, x_send, x_recv, z_tiles, y_send, y_recv,
-    w_first, w_second, b1_first, b1_second, b2_first, b2_second, basis_moved, f_send, f_recv,
+    w_first, w_second, b1_first, b1_second, b2_first, b2_second, basis_moved, f_rows, e_rows,
     local_sems, c_ssem, c_rsem, m_ssem, m_rsem, h_ssem, h_rsem, x_ssem, x_rsem, z_ssem, z_rsem,
-    y_ssem, y_rsem, w_ssem, w_rsem, b1_ssem, b1_rsem, b2_ssem, b2_rsem, f_ssem, f_rsem,
+    y_ssem, y_rsem, w_ssem, w_rsem, b1_ssem, b1_rsem, b2_ssem, b2_rsem, f_ssem, f_rsem, e_ssem, e_rsem,
 ):
     ws = (w_first, w_second)
     b1s = (b1_first, b1_second)
@@ -106,7 +105,7 @@
     own_copy.start()
 
     lane = lax.broadcasted_iota(jnp.int32, (R, GS), 1)
-    lane8 = lax.broadcasted_iota(jnp.int32, (8, GS), 1)
+    rotor = lax.broadcasted_iota(jnp.int32, (R, GS), 0)
     rows128 = lax.broadcasted_iota(jnp.int32, (8 * NV, GS), 0) // NV
     for load in loads:
         load.wait()
@@ -203,56 +202,37 @@
         wait_for(b2s[n].at[pl.ds(1, NZ - 1)], b2_rsem.at[n])
         return b2s[n][shift_z]
 
-    def rows_of(n):
-        return pl.ds(0, R if n == 0 else XROWS)
-
-    def send_x(n, coarse, inner):
-        x_send[n, pl.ds(0, R)] = coarse
-        if inner is not None:
-            x_send[n, pl.ds(R, 8)] = inner
-        for k in FAR_FIRST:
-            remote(
-                x_send.at[n, rows_of(n)], x_recv.at[n, k - 1, rows_of(n)],
-                x_ssem.at[n], x_rsem.at[n], x_peer(k),
-            )
+    def send_x(n, coarse):
+        x_send[n] = coarse
+        for k in FAR_FIRST:
+            remote(x_send.at[n], x_recv.at[n, k - 1], x_ssem.at[n], x_rsem.at[n], x_peer(k))
 
     def pass_z(n):
-        wait_for(x_recv.at[n, :, rows_of(n)], x_rsem.at[n])
-        total = x_send[n, rows_of(n)]
+        wait_for(x_recv.at[n], x_rsem.at[n])
+        total = x_send[n]
         for k in range(NAX - 1):
-            total = total + x_recv[n, k, rows_of(n)]
-        z_tiles[n, z, rows_of(n)] = total
-        for k in FAR_FIRST:
-            remote(
-                z_tiles.at[n, z, rows_of(n)], z_tiles.at[n, z, rows_of(n)],
-                z_ssem.at[n], z_rsem.at[n], z_peer(k),
-            )
+            total = total + x_recv[n, k]
+        z_tiles[n, z] = total
+        for k in FAR_FIRST:
+            remote(z_tiles.at[n, z], z_tiles.at[n, z], z_ssem.at[n], z_rsem.at[n], z_peer(k))
 
     def pass_y(n):
-        wait_for(z_tiles.at[n, pl.ds(0, NZ - 1), rows_of(n)], z_rsem.at[n])
-        gathered = jnp.concatenate([z_tiles[n, t, pl.ds(0, R)] for t in range(NZ)], axis=1)
+        wait_for(z_tiles.at[n, pl.ds(0, NZ - 1)], z_rsem.at[n])
+        gathered = jnp.concatenate([z_tiles[n, t] for t in range(NZ)], axis=1)
         if n == 0:
             own_copy.wait()
             wait_for(inverse_y.at[pl.ds(0, NY - 1)], m_rsem)
         matrix = jnp.concatenate([inverse_y[t] for t in range(NY)], axis=0)
-        y_send[n, pl.ds(0, R)] = joined(nt(two_parts(gathered), matrix))
-        if n > 0:
-            inner = z_tiles[n, 0, pl.ds(R, 8)]
-            for t in range(1, NZ):
-                inner = inner + z_tiles[n, t, pl.ds(R, 8)]
-            y_send[n, pl.ds(R, 8)] = inner
-        for k in FAR_FIRST:
-            remote(
-                y_send.at[n, rows_of(n)], y_recv.at[n, k - 1, rows_of(n)],
-                y_ssem.at[n], y_rsem.at[n], y_peer(k),
-            )
+        y_send[n] = joined(nt(two_parts(gathered), matrix))
+        for k in FAR_FIRST:
+            remote(y_send.at[n], y_recv.at[n, k - 1], y_ssem.at[n], y_rsem.at[n], y_peer(k))
 
     def get_y(n):
-        wait_for(y_recv.at[n, :, rows_of(n)], y_rsem.at[n])
-        total = y_send[n, rows_of(n)]
+        wait_for(y_recv.at[n], y_rsem.at[n])
+        total = y_send[n]
         for k in range(NY - 1):
-            total = total + y_recv[n, k, rows_of(n)]
-        return total[:R], total[R:]
+            total = total + y_recv[n, k]
+        return total
 
     def send_coarse(n, tile):
         ws[n][0] = tile
@@ -275,27 +255,49 @@
             square = square + image[a] * image[a]
         cross = jnp.sum(cross, axis=1, keepdims=True)
         square = jnp.sum(square, axis=1, keepdims=True)
-        tile = jnp.zeros((8, GS), F32)
-        for i, column in enumerate((cross[:8], square[:8], cross[8:], square[8:])):
-            tile = jnp.where(lane8 == i, column, tile)
-        return tile
-
-    def step_of(inner):
-        cross = jnp.concatenate([inner[:, 0:1], inner[:, 2:3]], axis=0)
-        square = jnp.concatenate([inner[:, 1:2], inner[:, 3:4]], axis=0)
+        spread_out = jnp.where(lane == rotor, cross, jnp.where(lane == rotor + R, square, 0.0))
+        return jnp.sum(spread_out, axis=0, keepdims=True)
+
+    def send_inner(n, row):
+        f_rows[n, pl.ds(NAX - 1, 1)] = row
+        for k in FAR_FIRST:
+            remote(
+                f_rows.at[n, pl.ds(NAX - 1, 1)], f_rows.at[n, pl.ds(k - 1, 1)],
+                f_ssem.at[n], f_rsem.at[n], x_peer(k),
+            )
+
+    def pass_inner(n):
+        wait_for(f_rows.at[n, pl.ds(0, NAX - 1)], f_rsem.at[n])
+        e_rows[n, pl.ds(NSEC - 1, 1)] = jnp.sum(f_rows[n], axis=0, keepdims=True)
+
+        def give(j, carry):
+            k = (j * 27) % NSEC
+            remote(
+                e_rows.at[n, pl.ds(NSEC - 1, 1)], e_rows.at[n, pl.ds(k - 1, 1)],
+                e_ssem.at[n], e_rsem.at[n], s_peer(k),
+            )
+            return carry
+
+        lax.fori_loop(1, NSEC, give, 0)
+
+    def get_step(n):
+        wait_for(e_rows.at[n, pl.ds(0, NSEC - 1)], e_rsem.at[n])
+        row = jnp.sum(e_rows[n], axis=0, keepdims=True)
+        cross = jnp.sum(jnp.where(lane == rotor, row, 0.0), axis=1, keepdims=True)
+        square = jnp.sum(jnp.where(lane == rotor + R, row, 0.0), axis=1, keepdims=True)
         return cross / (square + EPSILON)
 
     coarse_r0 = coarse_of(r0)
 
     pl.semaphore_wait(barrier, 7 + 7 + 7 + 2)
 
-    send_x(0, coarse_r0, None)
+    send_x(0, coarse_r0)
+    for k in FAR_FIRST:
+        remote(inverse_for((y + k) % NY), inverse_y.at[y], m_ssem, m_rsem, y_peer(k))
+    send_halo(0, r0)
     basis_moved[0] = basis[0].astype(BF16)
     for k in FAR_FIRST:
         remote(basis_moved.at[0], basis_moved.at[k], c_ssem, c_rsem, y_peer(k))
-    send_halo(0, r0)
-    for k in FAR_FIRST:
-        remote(inverse_for((y + k) % NY), inverse_y.at[y], m_ssem, m_rsem, y_peer(k))
     pass_z(0)
     halo_r0 = get_halo(0)
     solver_copy.wait()
@@ -303,7 +305,7 @@
     send_band(0, local_r0[0])
     pass_y(0)
     forward_band(0)
-    coarse, _ = get_y(0)
+    coarse = get_y(0)
     send_coarse(0, coarse)
     corr0 = [u + v for u, v in zip(local_r0, prolong(coarse, basis_y))]
     send_halo(1, corr0)
@@ -312,18 +314,20 @@
     band_corr0 = band_rows[:R] + prolong(get_coarse(0), band_basis)[0]
     image0 = apply_operator(corr0, get_halo(1), band_corr0)
 
-    send_x(1, coarse_of(image0), inner_products(r0, image0))
+    send_x(1, coarse_of(image0))
     send_halo(2, image0)
+    send_inner(0, inner_products(r0, image0))
     pass_z(1)
     local_im = local_solve(image0, get_halo(2))
     send_band(1, local_im[0])
+    pass_inner(0)
     pass_y(1)
     forward_band(1)
-    coarse, inner = get_y(1)
+    coarse = get_y(1)
     send_coarse(1, coarse)
     diff = [u + v for u, v in zip(local_im, prolong(coarse, basis_y))]
     send_halo(3, diff)
-    step0 = step_of(inner)
+    step0 = get_step(0)
     corr1 = [u - step0 * v for u, v in zip(corr0, diff)]
     res1 = [u - step0 * v for u, v in zip(r0, image0)]
     band_row = get_band(1)
@@ -331,52 +335,43 @@
     image_diff = apply_operator(diff, get_halo(3), band_diff)
     image1 = [u - step0 * v for u, v in zip(image0, image_diff)]
 
-    inner = inner_products(res1, image1)
-    for i, peer in enumerate((x_peer, y_peer, z_peer)):
-        f_send[i] = inner
-        for k in FAR_FIRST:
-            remote(f_send.at[i], f_recv.at[i, k - 1], f_ssem.at[i], f_rsem.at[i], peer(k))
-        wait_for(f_recv.at[i], f_rsem.at[i])
-        for k in range(7):
-            inner = inner + f_recv[i, k]
-    step1 = step_of(inner)
+    send_inner(1, inner_products(res1, image1))
+    pass_inner(1)
+    step1 = get_step(1)
     for a in range(GA):
-        sol_ref[:, a, :] = step0 * corr0[a] + step1 * corr1[a]
-        res_ref[:, a, :] = res1[a] - step1 * image1[a]
+        out_ref[0, :, a, :] = step0 * corr0[a] + step1 * corr1[a]
+        out_ref[1, :, a, :] = res1[a] - step1 * image1[a]
 
     wait_for(inverse_y.at[pl.ds(0, NY - 1)], m_ssem)
     wait_for(basis_moved.at[pl.ds(1, NY - 1)], c_ssem)
     for n in range(4):
         wait_for(h_recv.at[n], h_ssem.at[n])
     for n in range(2):
-        wait_for(x_recv.at[n, :, rows_of(n)], x_ssem.at[n])
-        wait_for(z_tiles.at[n, pl.ds(0, NZ - 1), rows_of(n)], z_ssem.at[n])
-        wait_for(y_recv.at[n, :, rows_of(n)], y_ssem.at[n])
+        wait_for(x_recv.at[n], x_ssem.at[n])
+        wait_for(z_tiles.at[n, pl.ds(0, NZ - 1)], z_ssem.at[n])
+        wait_for(y_recv.at[n], y_ssem.at[n])
         wait_for(ws[n].at[pl.ds(1, NZ - 1)], w_ssem.at[n])
         wait_for(b1s[n].at[pl.ds(1, NY - 1)], b1_ssem.at[n])
         wait_for(b2s[n].at[pl.ds(1, NZ - 1)], b2_ssem.at[n])
-    for i in range(3):
-        wait_for(f_recv.at[i], f_ssem.at[i])
+        wait_for(f_rows.at[n, pl.ds(0, NAX - 1)], f_ssem.at[n])
+        wait_for(e_rows.at[n, pl.ds(0, NSEC - 1)], e_ssem.at[n])
 
 
 def on_device(
     right_side, mass_term, band_weight, band_shift, local_solver, coarse_inverse, coarse_basis
 ):
-    vmem = pl.BlockSpec(memory_space=pltpu.VMEM)
-    smem = pl.BlockSpec(memory_space=pltpu.SMEM)
     hbm = pl.BlockSpec(memory_space=pltpu.HBM)
     dma = pltpu.SemaphoreType.DMA
-    out = jax.ShapeDtypeStruct(right_side.shape, F32)
 
     def tiles(*shape):
         return pltpu.VMEM(shape + (GS,), F32)
 
-    return pl.pallas_call(
+    both = pl.pallas_call(
         body,
         name="schwarz_steps",
-        out_shape=(out, out),
-        in_specs=[hbm, hbm, hbm, smem, hbm, hbm, hbm],
-        out_specs=(vmem, vmem),
+        out_shape=pltpu.VMEM((2,) + right_side.shape, F32),
+        in_specs=[hbm, hbm, hbm, pl.BlockSpec(memory_space=pltpu.SMEM), hbm, hbm, hbm],
+        out_specs=pl.BlockSpec(memory_space=pltpu.VMEM),
         scratch_shapes=[
             pltpu.VMEM(right_side.shape, F32),
             pltpu.VMEM(mass_term.shape, F32),
@@ -386,11 +381,11 @@
             pltpu.VMEM((NY, NV, NZ * GS), BF16),
             tiles(4, 3, R),
             tiles(4, 4, R),
-            tiles(2, XROWS),
-            tiles(2, NAX - 1, XROWS),
-            tiles(2, NZ, XROWS),
-            tiles(2, XROWS),
-            tiles(2, NY - 1, XROWS),
+            tiles(2, R),
+            tiles(2, NAX - 1, R),
+            tiles(2, NZ, R),
+            tiles(2, R),
+            tiles(2, NY - 1, R),
             tiles(NZ, R),
             tiles(NZ, R),
             tiles(NY, R),
@@ -398,8 +393,8 @@
             tiles(NZ, 2 * R),
             tiles(NZ, R),
             pltpu.VMEM((NY, NV, GS), BF16),
-            tiles(3, 8),
-            tiles(3, 7, 8),
+            tiles(2, NAX),
+            tiles(2, NSEC),
             dma((6,)),
             dma,
             dma,
@@ -408,8 +403,7 @@
             dma((4,)),
             dma((4,)),
         ]
-        + [dma((2,))] * 12
-        + [dma((3,))] * 2,
+        + [dma((2,))] * 16,
         compiler_params=pltpu.CompilerParams(
             collective_id=0, has_side_effects=True, vmem_limit_bytes=60 << 20
         ),
@@ -417,6 +411,7 @@
         right_side, mass_term, band_weight, band_shift, coarse_basis,
         jnp.swapaxes(local_solver, 1, 2), coarse_inverse,
     )
+    return both[0], both[1]
 
 
 def solution(mesh):

time: 68.4 us -> 66.2 us (0.968)
  local copies, waits for them, and re-layouts: 2 us -> 0.63 us
  Pallas kernels: 64.8 us -> 64.1 us
    unnamed x4 -> x0, local copies, waits for them, and re-layouts: 2 us -> none
    pallas_call x1, Pallas kernels: 64.8 us -> 64.1 us  [on_device(): pl.pallas_call(body, name='schwarz_steps', out_shape=pltpu.VMEM((2,) + ri...]
where the time goes in v4:
time: 66.2 us; the launch traced here: 66 us
  Pallas kernels  64.1 us (97%)
  between operations  1.28 us (2%)
    pallas_call x1, Pallas kernels, on_device(): pl.pallas_call(body, name='schwarz_steps', out_shape=pltpu.VMEM((2,) + ri...  64.1 us

profile of v4, /device:TPU:1, one launch (start us, length us, event | category | flops | bytes accessed | tf_op | source)
XLA Modules:
  0.0 66.0 jit_solution(11487141903139886119)
XLA Ops:
  1.3 64.1 %schwarz_steps.1 = f32[2,16,4,128]{3,2,1,0:T(4,128)S(1)} custom-call(f32[16,4,128]{2,1,0:T(4,128)} %rhs_hbm.1, f32[4,128]{1,0:T(4,128)} %mass_hbm.1, f32[1,128]{1,0:T(1,128)} %bw_hbm.1, s32[1]{0:T(128)S(6)} %copy.9.shift_ref, bf16[16,4,128]{2,1,0:T(4,128)(2,1)} %basis_hbm.1, bf16[1,780,512]{2,1,0:T(8,128)(2,1)} %bitcast.5, bf16[16,8192]{1,0:T(8,128)(2,1)} %inverse_hbm.1), custom_call_target="tpu_custom_call" | custom-call | tf_op jit(solution)/shard_map/schwarz_steps/pallas_call | solution.py:369
  65.4 0.6 slice_bitcast_fusion

commit v5 on v4

--- a/solution.py
+++ b/solution.py
@@ -46,8 +46,8 @@
     out_ref,
     rhs_ref, mass_ref, bw_ref, basis_ref,
     solver, inverse_y, h_send, h_recv, x_send, x_recv, z_tiles, y_send, y_recv,
-    w_first, w_second, b1_first, b1_second, b2_first, b2_second, basis_moved, f_rows, e_rows,
-    local_sems, c_ssem, c_rsem, m_ssem, m_rsem, h_ssem, h_rsem, x_ssem, x_rsem, z_ssem, z_rsem,
+    w_first, w_second, b1_first, b1_second, b2_first, b2_second, c1, c2, f_rows, e_rows,
+    local_sems, c1_ssem, c1_rsem, c2_ssem, c2_rsem, m_ssem, m_rsem, h_ssem, h_rsem, x_ssem, x_rsem, z_ssem, z_rsem,
     y_ssem, y_rsem, w_ssem, w_rsem, b1_ssem, b1_rsem, b2_ssem, b2_rsem, f_ssem, f_rsem, e_ssem, e_rsem,
 ):
     ws = (w_first, w_second)
@@ -184,23 +184,24 @@
             image.append(value)
         return image
 
+    def send_rows(slots, first, ssem, rsem, peer):
+        slots[0] = first
+        for k in FAR_FIRST:
+            remote(slots.at[0], slots.at[k], ssem, rsem, peer(k))
+
+    def get_rows(slots, sem, at):
+        wait_for(slots.at[pl.ds(1, 7)], sem)
+        return slots[at]
+
     def send_band(n, rows):
-        b1s[n][0] = rows
-        for k in FAR_FIRST:
-            remote(b1s[n].at[0], b1s[n].at[k], b1_ssem.at[n], b1_rsem.at[n], y_peer(k))
+        send_rows(b1s[n], rows, b1_ssem.at[n], b1_rsem.at[n], z_peer if n == 0 else y_peer)
 
     def forward_band(n):
-        wait_for(b1s[n].at[pl.ds(1, NY - 1)], b1_rsem.at[n])
-        b2s[n][0, pl.ds(0, R)] = b1s[n][up_there]
-        if n == 0:
-            wait_for(basis_moved.at[pl.ds(1, NY - 1)], c_rsem)
-            b2s[n][0, pl.ds(R, R)] = basis_moved[up_there].astype(F32)
-        for k in FAR_FIRST:
-            remote(b2s[n].at[0], b2s[n].at[k], b2_ssem.at[n], b2_rsem.at[n], z_peer(k))
+        row = get_rows(b1s[n], b1_rsem.at[n], shift_z if n == 0 else up_there)
+        send_rows(b2s[n], row, b2_ssem.at[n], b2_rsem.at[n], y_peer if n == 0 else z_peer)
 
     def get_band(n):
-        wait_for(b2s[n].at[pl.ds(1, NZ - 1)], b2_rsem.at[n])
-        return b2s[n][shift_z]
+        return get_rows(b2s[n], b2_rsem.at[n], up if n == 0 else shift_z)
 
     def send_x(n, coarse):
         x_send[n] = coarse
@@ -270,15 +271,13 @@
         wait_for(f_rows.at[n, pl.ds(0, NAX - 1)], f_rsem.at[n])
         e_rows[n, pl.ds(NSEC - 1, 1)] = jnp.sum(f_rows[n], axis=0, keepdims=True)
 
-        def give(j, carry):
-            k = (j * 27) % NSEC
-            remote(
-                e_rows.at[n, pl.ds(NSEC - 1, 1)], e_rows.at[n, pl.ds(k - 1, 1)],
-                e_ssem.at[n], e_rsem.at[n], s_peer(k),
-            )
-            return carry
-
-        lax.fori_loop(1, NSEC, give, 0)
+        for i in FAR_FIRST + (0,):
+            for j in FAR_FIRST + (0,):
+                if i or j:
+                    remote(
+                        e_rows.at[n, pl.ds(NSEC - 1, 1)], e_rows.at[n, pl.ds(i * NZ + j - 1, 1)],
+                        e_ssem.at[n], e_rsem.at[n], ((y + i) % NY * NZ + (z + j) % NZ, q),
+                    )
 
     def get_step(n):
         wait_for(e_rows.at[n, pl.ds(0, NSEC - 1)], e_rsem.at[n])
@@ -292,12 +291,10 @@
     pl.semaphore_wait(barrier, 7 + 7 + 7 + 2)
 
     send_x(0, coarse_r0)
+    send_halo(0, r0)
     for k in FAR_FIRST:
         remote(inverse_for((y + k) % NY), inverse_y.at[y], m_ssem, m_rsem, y_peer(k))
-    send_halo(0, r0)
-    basis_moved[0] = basis[0].astype(BF16)
-    for k in FAR_FIRST:
-        remote(basis_moved.at[0], basis_moved.at[k], c_ssem, c_rsem, y_peer(k))
+    send_rows(c1, basis[0].astype(BF16), c1_ssem, c1_rsem, z_peer)
     pass_z(0)
     halo_r0 = get_halo(0)
     solver_copy.wait()
@@ -305,13 +302,14 @@
     send_band(0, local_r0[0])
     pass_y(0)
     forward_band(0)
+    send_rows(c2, get_rows(c1, c1_rsem, shift_z), c2_ssem, c2_rsem, y_peer)
     coarse = get_y(0)
     send_coarse(0, coarse)
     corr0 = [u + v for u, v in zip(local_r0, prolong(coarse, basis_y))]
     send_halo(1, corr0)
-    band_rows = get_band(0)
-    band_basis = spread(band_rows[R:], (y + NY - up) % NY)
-    band_corr0 = band_rows[:R] + prolong(get_coarse(0), band_basis)[0]
+    band_row = get_band(0)
+    band_basis = spread(get_rows(c2, c2_rsem, up).astype(F32), (y + NY - up) % NY)
+    band_corr0 = band_row + prolong(get_coarse(0), band_basis)[0]
     image0 = apply_operator(corr0, get_halo(1), band_corr0)
 
     send_x(1, coarse_of(image0))
@@ -343,7 +341,8 @@
         out_ref[1, :, a, :] = res1[a] - step1 * image1[a]
 
     wait_for(inverse_y.at[pl.ds(0, NY - 1)], m_ssem)
-    wait_for(basis_moved.at[pl.ds(1, NY - 1)], c_ssem)
+    wait_for(c1.at[pl.ds(1, 7)], c1_ssem)
+    wait_for(c2.at[pl.ds(1, 7)], c2_ssem)
     for n in range(4):
         wait_for(h_recv.at[n], h_ssem.at[n])
     for n in range(2):
@@ -390,12 +389,15 @@
             tiles(NZ, R),
             tiles(NY, R),
             tiles(NY, R),
-            tiles(NZ, 2 * R),
+            tiles(NY, R),
             tiles(NZ, R),
+            pltpu.VMEM((NZ, NV, GS), BF16),
             pltpu.VMEM((NY, NV, GS), BF16),
             tiles(2, NAX),
             tiles(2, NSEC),
             dma((6,)),
+            dma,
+            dma,
             dma,
             dma,
             dma,

time: 66.2 us -> 63.6 us (0.961)
  Pallas kernels: 64.1 us -> 61.5 us
    pallas_call x1, Pallas kernels: 64.1 us -> 61.5 us  [on_device(): pl.pallas_call(body, name='schwarz_steps', out_shape=pltpu.VMEM((2,) + ri...]
where the time goes in v5:
time: 63.6 us; the launch traced here: 63.4 us
  Pallas kernels  61.5 us (97%)
  between operations  1.28 us (2%)
    pallas_call x1, Pallas kernels, on_device(): pl.pallas_call(body, name='schwarz_steps', out_shape=pltpu.VMEM((2,) + ri...  61.5 us

profile of v5, /device:TPU:1, one launch (start us, length us, event | category | flops | bytes accessed | tf_op | source)
XLA Modules:
  0.0 63.4 jit_solution(10112827877287897370)
XLA Ops:
  1.3 61.5 %schwarz_steps.1 = f32[2,16,4,128]{3,2,1,0:T(4,128)S(1)} custom-call(f32[16,4,128]{2,1,0:T(4,128)} %rhs_hbm.1, f32[4,128]{1,0:T(4,128)} %mass_hbm.1, f32[1,128]{1,0:T(1,128)} %bw_hbm.1, s32[1]{0:T(128)S(6)} %copy.9.shift_ref, bf16[16,4,128]{2,1,0:T(4,128)(2,1)} %basis_hbm.1, bf16[1,780,512]{2,1,0:T(8,128)(2,1)} %bitcast.5, bf16[16,8192]{1,0:T(8,128)(2,1)} %inverse_hbm.1), custom_call_target="tpu_custom_call" | custom-call | tf_op jit(solution)/shard_map/schwarz_steps/pallas_call | solution.py:368
  62.8 0.6 slice_bitcast_fusion

commit v6 on v5

--- a/solution.py
+++ b/solution.py
@@ -45,9 +45,9 @@
     rhs_hbm, mass_hbm, bw_hbm, shift_ref, basis_hbm, solver_hbm, inverse_hbm,
     out_ref,
     rhs_ref, mass_ref, bw_ref, basis_ref,
-    solver, inverse_y, h_send, h_recv, x_send, x_recv, z_tiles, y_send, y_recv,
+    solver, inverse_y, h_send, h_recv, x_send, x_recv, z_tiles, plane, y_send, y_recv,
     w_first, w_second, b1_first, b1_second, b2_first, b2_second, c1, c2, f_rows, e_rows,
-    local_sems, c1_ssem, c1_rsem, c2_ssem, c2_rsem, m_ssem, m_rsem, h_ssem, h_rsem, x_ssem, x_rsem, z_ssem, z_rsem,
+    local_sems, c1_ssem, c1_rsem, c2_ssem, c2_rsem, m_ssem, m_rsem, h_ssem, h_rsem, x_ssem, x_rsem, z_ssem, z_rsem, p_ssem, p_rsem,
     y_ssem, y_rsem, w_ssem, w_rsem, b1_ssem, b1_rsem, b2_ssem, b2_rsem, f_ssem, f_rsem, e_ssem, e_rsem,
 ):
     ws = (w_first, w_second)
@@ -106,6 +106,8 @@
 
     lane = lax.broadcasted_iota(jnp.int32, (R, GS), 1)
     rotor = lax.broadcasted_iota(jnp.int32, (R, GS), 0)
+    lane8 = lax.broadcasted_iota(jnp.int32, (8, GS), 1)
+    row8 = lax.broadcasted_iota(jnp.int32, (8, GS), 0)
     rows128 = lax.broadcasted_iota(jnp.int32, (8 * NV, GS), 0) // NV
     for load in loads:
         load.wait()
@@ -124,10 +126,24 @@
         return jnp.where(rows128 == at, jnp.concatenate([tile] * 8, axis=0), 0.0).astype(BF16)
 
     basis_q = jnp.concatenate([spread(t, q) for t in basis], axis=1)
+    basis_each = jnp.concatenate([jnp.concatenate([t] * 8, axis=0).astype(BF16) for t in basis], axis=1)
     basis_y = jnp.concatenate([spread(t, y) for t in basis], axis=1)
 
     def coarse_of(field):
         return joined(nt(two_parts(jnp.concatenate(field, axis=1)), basis_q))
+
+    def packed(tile):
+        kept = jnp.where(lane // NV == rotor % 8, tile, 0.0)
+        return [jnp.sum(kept[8 * h : 8 * h + 8], axis=0, keepdims=True) for h in range(2)]
+
+    def block_transposed(x):
+        for d in (4, 2, 1):
+            from_above = pltpu.roll(pltpu.roll(x, d, 0), GS - NV * d, 1)
+            from_below = pltpu.roll(pltpu.roll(x, 8 - d, 0), NV * d, 1)
+            row_bit = (row8 // d) % 2
+            block_bit = (lane8 // (NV * d)) % 2
+            x = jnp.where(row_bit == block_bit, x, jnp.where(row_bit == 1, from_above, from_below))
+        return x
 
     def edges(field):
         tile = jnp.zeros((R, GS), F32)
@@ -203,26 +219,48 @@
     def get_band(n):
         return get_rows(b2s[n], b2_rsem.at[n], up if n == 0 else shift_z)
 
-    def send_x(n, coarse):
-        x_send[n] = coarse
-        for k in FAR_FIRST:
-            remote(x_send.at[n], x_recv.at[n, k - 1], x_ssem.at[n], x_rsem.at[n], x_peer(k))
-
-    def pass_z(n):
-        wait_for(x_recv.at[n], x_rsem.at[n])
-        total = x_send[n]
+    def send_x(coarse):
+        x_send[...] = coarse
+        for k in FAR_FIRST:
+            remote(x_send, x_recv.at[k - 1], x_ssem, x_rsem, x_peer(k))
+
+    def pass_z():
+        wait_for(x_recv, x_rsem)
+        total = x_send[...]
         for k in range(NAX - 1):
-            total = total + x_recv[n, k]
-        z_tiles[n, z] = total
-        for k in FAR_FIRST:
-            remote(z_tiles.at[n, z], z_tiles.at[n, z], z_ssem.at[n], z_rsem.at[n], z_peer(k))
-
-    def pass_y(n):
-        wait_for(z_tiles.at[n, pl.ds(0, NZ - 1)], z_rsem.at[n])
-        gathered = jnp.concatenate([z_tiles[n, t] for t in range(NZ)], axis=1)
-        if n == 0:
-            own_copy.wait()
-            wait_for(inverse_y.at[pl.ds(0, NY - 1)], m_rsem)
+            total = total + x_recv[k]
+        z_tiles[z] = total
+        for k in FAR_FIRST:
+            remote(z_tiles.at[z], z_tiles.at[z], z_ssem, z_rsem, z_peer(k))
+
+    def get_z():
+        wait_for(z_tiles.at[pl.ds(0, NZ - 1)], z_rsem)
+        own_copy.wait()
+        wait_for(inverse_y.at[pl.ds(0, NY - 1)], m_rsem)
+        return jnp.concatenate([z_tiles[t] for t in range(NZ)], axis=1)
+
+    def send_plane(field):
+        out = joined(nt(two_parts(jnp.concatenate(field, axis=1)), basis_each))
+        at = z * NAX + q
+        for h, row in enumerate(packed(out)):
+            plane[h, pl.ds(at, 1)] = row
+        for j in FAR_FIRST + (0,):
+            for i in FAR_FIRST + (0,):
+                if i or j:
+                    remote(
+                        plane.at[:, pl.ds(at, 1)], plane.at[:, pl.ds(at, 1)],
+                        p_ssem, p_rsem, (y * NZ + (z + j) % NZ, (q + i) % NAX),
+                    )
+
+    def get_plane():
+        wait_for(plane.at[:, pl.ds(0, NZ * NAX - 1)], p_rsem)
+        halves = [
+            jnp.concatenate([block_transposed(plane[h, pl.ds(8 * t, 8)]) for t in range(NZ)], axis=1)
+            for h in range(2)
+        ]
+        return jnp.concatenate(halves, axis=0)
+
+    def pass_y(n, gathered):
         matrix = jnp.concatenate([inverse_y[t] for t in range(NY)], axis=0)
         y_send[n] = joined(nt(two_parts(gathered), matrix))
         for k in FAR_FIRST:
@@ -290,17 +328,17 @@
 
     pl.semaphore_wait(barrier, 7 + 7 + 7 + 2)
 
-    send_x(0, coarse_r0)
+    send_x(coarse_r0)
     send_halo(0, r0)
     for k in FAR_FIRST:
         remote(inverse_for((y + k) % NY), inverse_y.at[y], m_ssem, m_rsem, y_peer(k))
     send_rows(c1, basis[0].astype(BF16), c1_ssem, c1_rsem, z_peer)
-    pass_z(0)
+    pass_z()
     halo_r0 = get_halo(0)
     solver_copy.wait()
     local_r0 = local_solve(r0, halo_r0)
     send_band(0, local_r0[0])
-    pass_y(0)
+    pass_y(0, get_z())
     forward_band(0)
     send_rows(c2, get_rows(c1, c1_rsem, shift_z), c2_ssem, c2_rsem, y_peer)
     coarse = get_y(0)
@@ -312,14 +350,13 @@
     band_corr0 = band_row + prolong(get_coarse(0), band_basis)[0]
     image0 = apply_operator(corr0, get_halo(1), band_corr0)
 
-    send_x(1, coarse_of(image0))
+    send_plane(image0)
     send_halo(2, image0)
     send_inner(0, inner_products(r0, image0))
-    pass_z(1)
     local_im = local_solve(image0, get_halo(2))
     send_band(1, local_im[0])
     pass_inner(0)
-    pass_y(1)
+    pass_y(1, get_plane())
     forward_band(1)
     coarse = get_y(1)
     send_coarse(1, coarse)
@@ -343,11 +380,12 @@
     wait_for(inverse_y.at[pl.ds(0, NY - 1)], m_ssem)
     wait_for(c1.at[pl.ds(1, 7)], c1_ssem)
     wait_for(c2.at[pl.ds(1, 7)], c2_ssem)
+    wait_for(x_recv, x_ssem)
+    wait_for(z_tiles.at[pl.ds(0, NZ - 1)], z_ssem)
+    wait_for(plane.at[:, pl.ds(0, NZ * NAX - 1)], p_ssem)
     for n in range(4):
         wait_for(h_recv.at[n], h_ssem.at[n])
     for n in range(2):
-        wait_for(x_recv.at[n], x_ssem.at[n])
-        wait_for(z_tiles.at[n, pl.ds(0, NZ - 1)], z_ssem.at[n])
         wait_for(y_recv.at[n], y_ssem.at[n])
         wait_for(ws[n].at[pl.ds(1, NZ - 1)], w_ssem.at[n])
         wait_for(b1s[n].at[pl.ds(1, NY - 1)], b1_ssem.at[n])
@@ -380,9 +418,10 @@
             pltpu.VMEM((NY, NV, NZ * GS), BF16),
             tiles(4, 3, R),
             tiles(4, 4, R),
-            tiles(2, R),
-            tiles(2, NAX - 1, R),
-            tiles(2, NZ, R),
+            tiles(R),
+            tiles(NAX - 1, R),
+            tiles(NZ, R),
+            tiles(2, NZ * NAX),
             tiles(2, R),
             tiles(2, NY - 1, R),
             tiles(NZ, R),
@@ -405,7 +444,8 @@
             dma((4,)),
             dma((4,)),
         ]
-        + [dma((2,))] * 16,
+        + [dma] * 6
+        + [dma((2,))] * 12,
         compiler_params=pltpu.CompilerParams(
             collective_id=0, has_side_effects=True, vmem_limit_bytes=60 << 20
         ),

time: 63.6 us -> 61.8 us (0.972)
  Pallas kernels: 61.5 us -> 59.7 us
    pallas_call x1, Pallas kernels: 61.5 us -> 59.7 us  [on_device(): pl.pallas_call(body, name='schwarz_steps', out_shape=pltpu.VMEM((2,) + ri...]
where the time goes in v6:
time: 61.8 us; the launch traced here: 61.6 us
  Pallas kernels  59.7 us (97%)
  between operations  1.28 us (2%)
  local copies, waits for them, and re-layouts  0.63 us (1%)
    pallas_call x1, Pallas kernels, on_device(): pl.pallas_call(body, name='schwarz_steps', out_shape=pltpu.VMEM((2,) + ri...  59.7 us

profile of v6, /device:TPU:1, one launch (start us, length us, event | category | flops | bytes accessed | tf_op | source)
XLA Modules:
  0.0 61.6 jit_solution(3622876555251538761)
XLA Ops:
  1.3 59.7 %schwarz_steps.1 = f32[2,16,4,128]{3,2,1,0:T(4,128)S(1)} custom-call(f32[16,4,128]{2,1,0:T(4,128)} %rhs_hbm.1, f32[4,128]{1,0:T(4,128)} %mass_hbm.1, f32[1,128]{1,0:T(1,128)} %bw_hbm.1, s32[1]{0:T(128)S(6)} %copy.9.shift_ref, bf16[16,4,128]{2,1,0:T(4,128)(2,1)} %basis_hbm.1, bf16[1,780,512]{2,1,0:T(8,128)(2,1)} %bitcast.5, bf16[16,8192]{1,0:T(8,128)(2,1)} %inverse_hbm.1), custom_call_target="tpu_custom_call" | custom-call | tf_op jit(solution)/shard_map/schwarz_steps/pallas_call | solution.py:406
  61.0 0.6 %slice_bitcast_fusion = (f32[16,4,128]{2,1,0:T(4,128)}, f32[16,4,128]{2,1,0:T(4,128)}) fusion(f32[2,16,4,128]{3,2,1,0:T(4,128)S(1)} %schwarz_steps.1), kind=kLoop, calls=%fused_computation | loop fusion | bytes 131072 | tf_op jit(solution)/shard_map/squeeze | solution.py:456

commit v7 on v6

--- a/solution.py
+++ b/solution.py
@@ -45,12 +45,12 @@
     rhs_hbm, mass_hbm, bw_hbm, shift_ref, basis_hbm, solver_hbm, inverse_hbm,
     out_ref,
     rhs_ref, mass_ref, bw_ref, basis_ref,
-    solver, inverse_y, h_send, h_recv, x_send, x_recv, z_tiles, plane, y_send, y_recv,
-    w_first, w_second, b1_first, b1_second, b2_first, b2_second, c1, c2, f_rows, e_rows,
+    solver, inverse_y, h_send, h_recv, x_send, x_recv, z_tiles, plane, shares, beside,
+    got_first, got_second, b1_first, b1_second, b2_first, b2_second, c1, c2, f_rows, e_rows,
     local_sems, c1_ssem, c1_rsem, c2_ssem, c2_rsem, m_ssem, m_rsem, h_ssem, h_rsem, x_ssem, x_rsem, z_ssem, z_rsem, p_ssem, p_rsem,
-    y_ssem, y_rsem, w_ssem, w_rsem, b1_ssem, b1_rsem, b2_ssem, b2_rsem, f_ssem, f_rsem, e_ssem, e_rsem,
+    s_ssem, s_rsem, r_ssem, r_rsem, a_ssem, a_rsem, b1_ssem, b1_rsem, b2_ssem, b2_rsem, f_ssem, f_rsem, e_ssem, e_rsem,
 ):
-    ws = (w_first, w_second)
+    got = (got_first, got_second)
     b1s = (b1_first, b1_second)
     b2s = (b2_first, b2_second)
     s = lax.axis_index("sector")
@@ -125,9 +125,11 @@
     def spread(tile, at):
         return jnp.where(rows128 == at, jnp.concatenate([tile] * 8, axis=0), 0.0).astype(BF16)
 
+    def each(tile):
+        return jnp.concatenate([tile.astype(F32)] * 8, axis=0).astype(BF16)
+
     basis_q = jnp.concatenate([spread(t, q) for t in basis], axis=1)
-    basis_each = jnp.concatenate([jnp.concatenate([t] * 8, axis=0).astype(BF16) for t in basis], axis=1)
-    basis_y = jnp.concatenate([spread(t, y) for t in basis], axis=1)
+    basis_each = jnp.concatenate([each(t) for t in basis], axis=1)
 
     def coarse_of(field):
         return joined(nt(two_parts(jnp.concatenate(field, axis=1)), basis_q))
@@ -260,27 +262,55 @@
         ]
         return jnp.concatenate(halves, axis=0)
 
-    def pass_y(n, gathered):
+    def send_shares(n, gathered):
         matrix = jnp.concatenate([inverse_y[t] for t in range(NY)], axis=0)
-        y_send[n] = joined(nt(two_parts(gathered), matrix))
-        for k in FAR_FIRST:
-            remote(y_send.at[n], y_recv.at[n, k - 1], y_ssem.at[n], y_rsem.at[n], y_peer(k))
-
-    def get_y(n):
-        wait_for(y_recv.at[n], y_rsem.at[n])
-        total = y_send[n]
-        for k in range(NY - 1):
-            total = total + y_recv[n, k]
-        return total
-
-    def send_coarse(n, tile):
-        ws[n][0] = tile
-        for k in FAR_FIRST:
-            remote(ws[n].at[0], ws[n].at[k], w_ssem.at[n], w_rsem.at[n], z_peer(k))
-
-    def get_coarse(n):
-        wait_for(ws[n].at[pl.ds(1, NZ - 1)], w_rsem.at[n])
-        return ws[n][shift_z]
+        out = joined(nt(two_parts(gathered), matrix))
+        for h in range(2):
+            share = block_transposed(out[8 * h : 8 * h + 8])
+            band = pltpu.roll(share, up_there, 0)
+            ahead = jnp.where(z == NZ - 1, pltpu.roll(share, 1, 0), share)
+            behind = jnp.where(z == 0, pltpu.roll(share, NY - 1, 0), share)
+            for i, own in enumerate((share, ahead, behind)):
+                shares[n, i, h] = own
+                shares[n, i, 2 + h] = band
+        for h in range(4):
+            got[n][h, z, pl.ds(y, 1)] = shares[n, 0, h, pl.ds(y, 1)]
+        for i in FAR_FIRST + (0,):
+            to = (y + i) % NY
+            for j in FAR_FIRST + (0,):
+                if i or j:
+                    remote(
+                        shares.at[n, {1: 1, NZ - 1: 2}.get(j, 0), :, pl.ds(to, 1)], got[n].at[:, z, pl.ds(y, 1)],
+                        (s_ssem if j else r_ssem).at[n], (s_rsem if j else r_rsem).at[n],
+                        (to * NZ + (z + j) % NZ, q),
+                    )
+            for side, k in enumerate((1, NAX - 1)):
+                remote(
+                    shares.at[n, 0, pl.ds(0, 2), pl.ds(to, 1)], beside.at[n, side, :, pl.ds(y, 1)],
+                    a_ssem.at[n], a_rsem.at[n], (to * NZ + z, (q + k) % NAX),
+                )
+
+    def wait_shares(n, s_sem, r_sem, a_sem):
+        wait_for(got[n].at[:, pl.ds(0, NZ - 1)], s_sem.at[n])
+        wait_for(got[n].at[:, 0, pl.ds(0, NY - 1)], r_sem.at[n])
+        wait_for(beside.at[n], a_sem.at[n])
+
+    def unpacked(first, second):
+        rows = [jnp.sum(x, axis=0, keepdims=True) for x in (first, second)]
+        tile = jnp.concatenate([jnp.broadcast_to(x, (8, GS)) for x in rows], axis=0)
+        return jnp.where(lane // NV == rotor % 8, tile, 0.0)
+
+    def get_shares(n):
+        wait_shares(n, s_rsem, r_rsem, a_rsem)
+
+        def along_z(at, h=0):
+            return unpacked(got[n][h, at], got[n][h + 1, at])
+
+        sides = (
+            along_z((z + NZ - 1) % NZ), along_z((z + 1) % NZ),
+            unpacked(beside[n, 0, 0], beside[n, 0, 1]), unpacked(beside[n, 1, 0], beside[n, 1, 1]),
+        )
+        return along_z(z), sides, along_z((z + NZ - shift_z) % NZ, 2)
 
     def prolong(coarse, rows):
         out = joined(nn(two_parts(coarse), rows))
@@ -330,6 +360,7 @@
 
     send_x(coarse_r0)
     send_halo(0, r0)
+    send_halo(4, basis)
     for k in FAR_FIRST:
         remote(inverse_for((y + k) % NY), inverse_y.at[y], m_ssem, m_rsem, y_peer(k))
     send_rows(c1, basis[0].astype(BF16), c1_ssem, c1_rsem, z_peer)
@@ -338,36 +369,40 @@
     solver_copy.wait()
     local_r0 = local_solve(r0, halo_r0)
     send_band(0, local_r0[0])
-    pass_y(0, get_z())
+    send_halo(1, local_r0)
+    send_shares(0, get_z())
     forward_band(0)
     send_rows(c2, get_rows(c1, c1_rsem, shift_z), c2_ssem, c2_rsem, y_peer)
-    coarse = get_y(0)
-    send_coarse(0, coarse)
-    corr0 = [u + v for u, v in zip(local_r0, prolong(coarse, basis_y))]
-    send_halo(1, corr0)
+    basis_sides = [each(t) for t in get_halo(4)]
+    halo = get_halo(1)
     band_row = get_band(0)
-    band_basis = spread(get_rows(c2, c2_rsem, up).astype(F32), (y + NY - up) % NY)
-    band_corr0 = band_row + prolong(get_coarse(0), band_basis)[0]
-    image0 = apply_operator(corr0, get_halo(1), band_corr0)
+    band_basis = each(get_rows(c2, c2_rsem, up))
+
+    def with_coarse(field, halo, band_row, n):
+        coarse, sides, band = get_shares(n)
+        own = [u + v for u, v in zip(field, prolong(coarse, basis_each))]
+        around = [u + prolong(v, w)[0] for u, v, w in zip(halo, sides, basis_sides)]
+        return own, around, band_row + prolong(band, band_basis)[0]
+
+    corr0, halo, band_row = with_coarse(local_r0, halo, band_row, 0)
+    image0 = apply_operator(corr0, halo, band_row)
 
     send_plane(image0)
     send_halo(2, image0)
     send_inner(0, inner_products(r0, image0))
     local_im = local_solve(image0, get_halo(2))
     send_band(1, local_im[0])
+    send_halo(3, local_im)
     pass_inner(0)
-    pass_y(1, get_plane())
+    send_shares(1, get_plane())
     forward_band(1)
-    coarse = get_y(1)
-    send_coarse(1, coarse)
-    diff = [u + v for u, v in zip(local_im, prolong(coarse, basis_y))]
-    send_halo(3, diff)
     step0 = get_step(0)
+    res1 = [u - step0 * v for u, v in zip(r0, image0)]
+    halo = get_halo(3)
+    band_row = get_band(1)
+    diff, halo, band_row = with_coarse(local_im, halo, band_row, 1)
+    image_diff = apply_operator(diff, halo, band_row)
     corr1 = [u - step0 * v for u, v in zip(corr0, diff)]
-    res1 = [u - step0 * v for u, v in zip(r0, image0)]
-    band_row = get_band(1)
-    band_diff = band_row + prolong(get_coarse(1), band_basis)[0]
-    image_diff = apply_operator(diff, get_halo(3), band_diff)
     image1 = [u - step0 * v for u, v in zip(image0, image_diff)]
 
     send_inner(1, inner_products(res1, image1))
@@ -383,11 +418,10 @@
     wait_for(x_recv, x_ssem)
     wait_for(z_tiles.at[pl.ds(0, NZ - 1)], z_ssem)
     wait_for(plane.at[:, pl.ds(0, NZ * NAX - 1)], p_ssem)
-    for n in range(4):
+    for n in range(5):
         wait_for(h_recv.at[n], h_ssem.at[n])
     for n in range(2):
-        wait_for(y_recv.at[n], y_ssem.at[n])
-        wait_for(ws[n].at[pl.ds(1, NZ - 1)], w_ssem.at[n])
+        wait_shares(n, s_ssem, r_ssem, a_ssem)
         wait_for(b1s[n].at[pl.ds(1, NY - 1)], b1_ssem.at[n])
         wait_for(b2s[n].at[pl.ds(1, NZ - 1)], b2_ssem.at[n])
         wait_for(f_rows.at[n, pl.ds(0, NAX - 1)], f_ssem.at[n])
@@ -416,16 +450,16 @@
             pltpu.VMEM(coarse_basis.shape, BF16),
             pltpu.VMEM((NEXT, GA * GS), BF16),
             pltpu.VMEM((NY, NV, NZ * GS), BF16),
-            tiles(4, 3, R),
-            tiles(4, 4, R),
+            tiles(5, 3, R),
+            tiles(5, 4, R),
             tiles(R),
             tiles(NAX - 1, R),
             tiles(NZ, R),
             tiles(2, NZ * NAX),
-            tiles(2, R),
-            tiles(2, NY - 1, R),
-            tiles(NZ, R),
-            tiles(NZ, R),
+            tiles(2, 3, 4, NY),
+            tiles(2, 2, 2, NY),
+            tiles(4, NZ, NY),
+            tiles(4, NZ, NY),
             tiles(NY, R),
             tiles(NY, R),
             tiles(NY, R),
@@ -441,11 +475,11 @@
             dma,
             dma,
             dma,
-            dma((4,)),
-            dma((4,)),
+            dma((5,)),
+            dma((5,)),
         ]
         + [dma] * 6
-        + [dma((2,))] * 12,
+        + [dma((2,))] * 14,
         compiler_params=pltpu.CompilerParams(
             collective_id=0, has_side_effects=True, vmem_limit_bytes=60 << 20
         ),

time: 61.8 us -> 60 us (0.971)
  Pallas kernels: 59.7 us -> 57.9 us
    pallas_call x1, Pallas kernels: 59.7 us -> 57.9 us  [on_device(): pl.pallas_call(body, name='schwarz_steps', out_shape=pltpu.VMEM((2,) + ri...]
where the time goes in v7:
time: 60 us; the launch traced here: 59.8 us
  Pallas kernels  57.9 us (96%)
  between operations  1.28 us (2%)
  local copies, waits for them, and re-layouts  0.63 us (1%)
    pallas_call x1, Pallas kernels, on_device(): pl.pallas_call(body, name='schwarz_steps', out_shape=pltpu.VMEM((2,) + ri...  57.9 us

profile of v7, /device:TPU:1, one launch (start us, length us, event | category | flops | bytes accessed | tf_op | source)
XLA Modules:
  0.0 59.8 jit_solution(842587374832286508)
XLA Ops:
  1.3 57.9 %schwarz_steps.1 = f32[2,16,4,128]{3,2,1,0:T(4,128)S(1)} custom-call(f32[16,4,128]{2,1,0:T(4,128)} %rhs_hbm.1, f32[4,128]{1,0:T(4,128)} %mass_hbm.1, f32[1,128]{1,0:T(1,128)} %bw_hbm.1, s32[1]{0:T(128)S(6)} %copy.9.shift_ref, bf16[16,4,128]{2,1,0:T(4,128)(2,1)} %basis_hbm.1, bf16[1,780,512]{2,1,0:T(8,128)(2,1)} %bitcast.5, bf16[16,8192]{1,0:T(8,128)(2,1)} %inverse_hbm.1), custom_call_target="tpu_custom_call" | custom-call | tf_op jit(solution)/shard_map/schwarz_steps/pallas_call | solution.py:440
  59.2 0.6 %slice_bitcast_fusion = (f32[16,4,128]{2,1,0:T(4,128)}, f32[16,4,128]{2,1,0:T(4,128)}) fusion(f32[2,16,4,128]{3,2,1,0:T(4,128)S(1)} %schwarz_steps.1), kind=kLoop, calls=%fused_computation | loop fusion | bytes 131072 | tf_op jit(solution)/shard_map/squeeze | solution.py:490

commit v8 on v7

--- a/solution.py
+++ b/solution.py
@@ -48,7 +48,7 @@
     solver, inverse_y, h_send, h_recv, x_send, x_recv, z_tiles, plane, shares, beside,
     got_first, got_second, b1_first, b1_second, b2_first, b2_second, c1, c2, f_rows, e_rows,
     local_sems, c1_ssem, c1_rsem, c2_ssem, c2_rsem, m_ssem, m_rsem, h_ssem, h_rsem, x_ssem, x_rsem, z_ssem, z_rsem, p_ssem, p_rsem,
-    s_ssem, s_rsem, r_ssem, r_rsem, a_ssem, a_rsem, b1_ssem, b1_rsem, b2_ssem, b2_rsem, f_ssem, f_rsem, e_ssem, e_rsem,
+    s_ssem, s_rsem, o_ssem, o_rsem, r_ssem, r_rsem, a_ssem, a_rsem, b1_ssem, b1_rsem, b2_ssem, b2_rsem, f_ssem, f_rsem, e_ssem, e_rsem,
 ):
     got = (got_first, got_second)
     b1s = (b1_first, b1_second)
@@ -278,11 +278,21 @@
         for i in FAR_FIRST + (0,):
             to = (y + i) % NY
             for j in FAR_FIRST + (0,):
-                if i or j:
+                sector = (to * NZ + (z + j) % NZ, q)
+                if j in (1, NZ - 1):
                     remote(
-                        shares.at[n, {1: 1, NZ - 1: 2}.get(j, 0), :, pl.ds(to, 1)], got[n].at[:, z, pl.ds(y, 1)],
-                        (s_ssem if j else r_ssem).at[n], (s_rsem if j else r_rsem).at[n],
-                        (to * NZ + (z + j) % NZ, q),
+                        shares.at[n, 1 if j == 1 else 2, :, pl.ds(to, 1)], got[n].at[:, z, pl.ds(y, 1)],
+                        s_ssem.at[n], s_rsem.at[n], sector,
+                    )
+                elif j:
+                    remote(
+                        shares.at[n, 0, pl.ds(2, 2), pl.ds(to, 1)], got[n].at[pl.ds(2, 2), z, pl.ds(y, 1)],
+                        o_ssem.at[n], o_rsem.at[n], sector,
+                    )
+                elif i:
+                    remote(
+                        shares.at[n, 0, :, pl.ds(to, 1)], got[n].at[:, z, pl.ds(y, 1)],
+                        r_ssem.at[n], r_rsem.at[n], sector,
                     )
             for side, k in enumerate((1, NAX - 1)):
                 remote(
@@ -290,8 +300,9 @@
                     a_ssem.at[n], a_rsem.at[n], (to * NZ + z, (q + k) % NAX),
                 )
 
-    def wait_shares(n, s_sem, r_sem, a_sem):
-        wait_for(got[n].at[:, pl.ds(0, NZ - 1)], s_sem.at[n])
+    def wait_shares(n, s_sem, o_sem, r_sem, a_sem):
+        wait_for(got[n].at[:, pl.ds(0, 2)], s_sem.at[n])
+        wait_for(got[n].at[pl.ds(0, 2), pl.ds(0, NZ - 3)], o_sem.at[n])
         wait_for(got[n].at[:, 0, pl.ds(0, NY - 1)], r_sem.at[n])
         wait_for(beside.at[n], a_sem.at[n])
 
@@ -301,7 +312,7 @@
         return jnp.where(lane // NV == rotor % 8, tile, 0.0)
 
     def get_shares(n):
-        wait_shares(n, s_rsem, r_rsem, a_rsem)
+        wait_shares(n, s_rsem, o_rsem, r_rsem, a_rsem)
 
         def along_z(at, h=0):
             return unpacked(got[n][h, at], got[n][h + 1, at])
@@ -370,9 +381,9 @@
     local_r0 = local_solve(r0, halo_r0)
     send_band(0, local_r0[0])
     send_halo(1, local_r0)
+    send_rows(c2, get_rows(c1, c1_rsem, shift_z), c2_ssem, c2_rsem, y_peer)
     send_shares(0, get_z())
     forward_band(0)
-    send_rows(c2, get_rows(c1, c1_rsem, shift_z), c2_ssem, c2_rsem, y_peer)
     basis_sides = [each(t) for t in get_halo(4)]
     halo = get_halo(1)
     band_row = get_band(0)
@@ -387,8 +398,8 @@
     corr0, halo, band_row = with_coarse(local_r0, halo, band_row, 0)
     image0 = apply_operator(corr0, halo, band_row)
 
+    send_halo(2, image0)
     send_plane(image0)
-    send_halo(2, image0)
     send_inner(0, inner_products(r0, image0))
     local_im = local_solve(image0, get_halo(2))
     send_band(1, local_im[0])
@@ -421,7 +432,7 @@
     for n in range(5):
         wait_for(h_recv.at[n], h_ssem.at[n])
     for n in range(2):
-        wait_shares(n, s_ssem, r_ssem, a_ssem)
+        wait_shares(n, s_ssem, o_ssem, r_ssem, a_ssem)
         wait_for(b1s[n].at[pl.ds(1, NY - 1)], b1_ssem.at[n])
         wait_for(b2s[n].at[pl.ds(1, NZ - 1)], b2_ssem.at[n])
         wait_for(f_rows.at[n, pl.ds(0, NAX - 1)], f_ssem.at[n])
@@ -479,7 +490,7 @@
             dma((5,)),
         ]
         + [dma] * 6
-        + [dma((2,))] * 14,
+        + [dma((2,))] * 16,
         compiler_params=pltpu.CompilerParams(
             collective_id=0, has_side_effects=True, vmem_limit_bytes=60 << 20
         ),

time: 60 us -> 58.7 us (0.978)
  Pallas kernels: 57.9 us -> 56.7 us
    pallas_call x1, Pallas kernels: 57.9 us -> 56.7 us  [on_device(): pl.pallas_call(body, name='schwarz_steps', out_shape=pltpu.VMEM((2,) + ri...]
where the time goes in v8:
time: 58.7 us; the launch traced here: 58.6 us
  Pallas kernels  56.7 us (97%)
  between operations  1.28 us (2%)
  local copies, waits for them, and re-layouts  0.63 us (1%)
    pallas_call x1, Pallas kernels, on_device(): pl.pallas_call(body, name='schwarz_steps', out_shape=pltpu.VMEM((2,) + ri...  56.7 us

profile of v8, /device:TPU:1, one launch (start us, length us, event | category | flops | bytes accessed | tf_op | source)
XLA Modules:
  0.0 58.6 jit_solution(11853397739954792259)
XLA Ops:
  1.3 56.7 %schwarz_steps.1 = f32[2,16,4,128]{3,2,1,0:T(4,128)S(1)} custom-call(f32[16,4,128]{2,1,0:T(4,128)} %rhs_hbm.1, f32[4,128]{1,0:T(4,128)} %mass_hbm.1, f32[1,128]{1,0:T(1,128)} %bw_hbm.1, s32[1]{0:T(128)S(6)} %copy.9.shift_ref, bf16[16,4,128]{2,1,0:T(4,128)(2,1)} %basis_hbm.1, bf16[1,780,512]{2,1,0:T(8,128)(2,1)} %bitcast.5, bf16[16,8192]{1,0:T(8,128)(2,1)} %inverse_hbm.1), custom_call_target="tpu_custom_call" | custom-call | tf_op jit(solution)/shard_map/schwarz_steps/pallas_call | solution.py:451
  58.0 0.6 %slice_bitcast_fusion = (f32[16,4,128]{2,1,0:T(4,128)}, f32[16,4,128]{2,1,0:T(4,128)}) fusion(f32[2,16,4,128]{3,2,1,0:T(4,128)S(1)} %schwarz_steps.1), kind=kLoop, calls=%fused_computation | loop fusion | bytes 131072 | tf_op jit(solution)/shard_map/squeeze | solution.py:501

commit v9 on v8

--- a/solution.py
+++ b/solution.py
@@ -79,6 +79,13 @@
             device_id=device, device_id_type=MESH,
         ).start()
 
+    barrier = pltpu.get_barrier_semaphore()
+    for k in FAR_FIRST:
+        for peer in (y_peer(k), z_peer(k), x_peer(k)):
+            pl.semaphore_signal(barrier, inc=1, device_id=peer, device_id_type=MESH)
+    for k in (1, NSEC - 1):
+        pl.semaphore_signal(barrier, inc=1, device_id=s_peer(k), device_id_type=MESH)
+
     loads = [
         pltpu.make_async_copy(src, dst, local_sems.at[i])
         for i, (src, dst) in enumerate(
@@ -87,14 +94,6 @@
     ]
     for load in loads:
         load.start()
-
-    barrier = pltpu.get_barrier_semaphore()
-    for k in FAR_FIRST:
-        for peer in (y_peer(k), z_peer(k), x_peer(k)):
-            pl.semaphore_signal(barrier, inc=1, device_id=peer, device_id_type=MESH)
-    for k in (1, NSEC - 1):
-        pl.semaphore_signal(barrier, inc=1, device_id=s_peer(k), device_id_type=MESH)
-
     solver_copy = pltpu.make_async_copy(solver_hbm.at[0], solver, local_sems.at[4])
     solver_copy.start()
 
@@ -129,7 +128,6 @@
         return jnp.concatenate([tile.astype(F32)] * 8, axis=0).astype(BF16)
 
     basis_q = jnp.concatenate([spread(t, q) for t in basis], axis=1)
-    basis_each = jnp.concatenate([each(t) for t in basis], axis=1)
 
     def coarse_of(field):
         return joined(nt(two_parts(jnp.concatenate(field, axis=1)), basis_q))
@@ -371,11 +369,12 @@
 
     send_x(coarse_r0)
     send_halo(0, r0)
-    send_halo(4, basis)
     for k in FAR_FIRST:
         remote(inverse_for((y + k) % NY), inverse_y.at[y], m_ssem, m_rsem, y_peer(k))
     send_rows(c1, basis[0].astype(BF16), c1_ssem, c1_rsem, z_peer)
+    send_halo(4, basis)
     pass_z()
+    basis_each = jnp.concatenate([each(t) for t in basis], axis=1)
     halo_r0 = get_halo(0)
     solver_copy.wait()
     local_r0 = local_solve(r0, halo_r0)

time: 58.7 us -> 58.6 us (level)
  no operation moved by 1% of the time
where the time goes in v9:
time: 58.6 us; the launch traced here: 58.5 us
  Pallas kernels  56.6 us (97%)
  between operations  1.28 us (2%)
  local copies, waits for them, and re-layouts  0.63 us (1%)
    pallas_call x1, Pallas kernels, on_device(): pl.pallas_call(body, name='schwarz_steps', out_shape=pltpu.VMEM((2,) + ri...  56.6 us

profile of v9, /device:TPU:1, one launch (start us, length us, event | category | flops | bytes accessed | tf_op | source)
XLA Modules:
  0.0 58.5 jit_solution(3284781418373212733)
XLA Ops:
  1.3 56.6 %schwarz_steps.1 = f32[2,16,4,128]{3,2,1,0:T(4,128)S(1)} custom-call(f32[16,4,128]{2,1,0:T(4,128)} %rhs_hbm.1, f32[4,128]{1,0:T(4,128)} %mass_hbm.1, f32[1,128]{1,0:T(1,128)} %bw_hbm.1, s32[1]{0:T(128)S(6)} %copy.9.shift_ref, bf16[16,4,128]{2,1,0:T(4,128)(2,1)} %basis_hbm.1, bf16[1,780,512]{2,1,0:T(8,128)(2,1)} %bitcast.5, bf16[16,8192]{1,0:T(8,128)(2,1)} %inverse_hbm.1), custom_call_target="tpu_custom_call" | custom-call | tf_op jit(solution)/shard_map/schwarz_steps/pallas_call | solution.py:450
  57.9 0.6 %slice_bitcast_fusion = (f32[16,4,128]{2,1,0:T(4,128)}, f32[16,4,128]{2,1,0:T(4,128)}) fusion(f32[2,16,4,128]{3,2,1,0:T(4,128)S(1)} %schwarz_steps.1), kind=kLoop, calls=%fused_computation | loop fusion | bytes 131072 | tf_op jit(solution)/shard_map/squeeze | solution.py:500

commit v10 on v9

--- a/solution.py
+++ b/solution.py
@@ -412,15 +412,12 @@
     band_row = get_band(1)
     diff, halo, band_row = with_coarse(local_im, halo, band_row, 1)
     image_diff = apply_operator(diff, halo, band_row)
-    corr1 = [u - step0 * v for u, v in zip(corr0, diff)]
     image1 = [u - step0 * v for u, v in zip(image0, image_diff)]
 
     send_inner(1, inner_products(res1, image1))
     pass_inner(1)
-    step1 = get_step(1)
-    for a in range(GA):
-        out_ref[0, :, a, :] = step0 * corr0[a] + step1 * corr1[a]
-        out_ref[1, :, a, :] = res1[a] - step1 * image1[a]
+    corr1 = [u - step0 * v for u, v in zip(corr0, diff)]
+    sol0 = [step0 * u for u in corr0]
 
     wait_for(inverse_y.at[pl.ds(0, NY - 1)], m_ssem)
     wait_for(c1.at[pl.ds(1, 7)], c1_ssem)
@@ -436,6 +433,11 @@
         wait_for(b2s[n].at[pl.ds(1, NZ - 1)], b2_ssem.at[n])
         wait_for(f_rows.at[n, pl.ds(0, NAX - 1)], f_ssem.at[n])
         wait_for(e_rows.at[n, pl.ds(0, NSEC - 1)], e_ssem.at[n])
+
+    step1 = get_step(1)
+    for a in range(GA):
+        out_ref[0, :, a, :] = sol0[a] + step1 * corr1[a]
+        out_ref[1, :, a, :] = res1[a] - step1 * image1[a]
 
 
 def on_device(

time: 58.6 us -> 58.6 us (level)
  no operation moved by 1% of the time
where the time goes in v10:
time: 58.6 us; the launch traced here: 58.5 us
  Pallas kernels  56.5 us (96%)
  between operations  1.28 us (2%)
  local copies, waits for them, and re-layouts  0.63 us (1%)
    pallas_call x1, Pallas kernels, on_device(): pl.pallas_call(body, name='schwarz_steps', out_shape=pltpu.VMEM((2,) + ri...  56.5 us

profile of v10, /device:TPU:1, one launch (start us, length us, event | category | flops | bytes accessed | tf_op | source)
XLA Modules:
  0.0 58.5 jit_solution(9925974231736119940)
XLA Ops:
  1.3 56.5 %schwarz_steps.1 = f32[2,16,4,128]{3,2,1,0:T(4,128)S(1)} custom-call(f32[16,4,128]{2,1,0:T(4,128)} %rhs_hbm.1, f32[4,128]{1,0:T(4,128)} %mass_hbm.1, f32[1,128]{1,0:T(1,128)} %bw_hbm.1, s32[1]{0:T(128)S(6)} %copy.9.shift_ref, bf16[16,4,128]{2,1,0:T(4,128)(2,1)} %basis_hbm.1, bf16[1,780,512]{2,1,0:T(8,128)(2,1)} %bitcast.5, bf16[16,8192]{1,0:T(8,128)(2,1)} %inverse_hbm.1), custom_call_target="tpu_custom_call" | custom-call | tf_op jit(solution)/shard_map/schwarz_steps/pallas_call | solution.py:452
  57.8 0.6 %slice_bitcast_fusion = (f32[16,4,128]{2,1,0:T(4,128)}, f32[16,4,128]{2,1,0:T(4,128)}) fusion(f32[2,16,4,128]{3,2,1,0:T(4,128)S(1)} %schwarz_steps.1), kind=kLoop, calls=%fused_computation | loop fusion | bytes 131072 | tf_op jit(solution)/shard_map/squeeze | solution.py:502

commit v11 on v10

--- a/solution.py
+++ b/solution.py
@@ -372,8 +372,8 @@
     for k in FAR_FIRST:
         remote(inverse_for((y + k) % NY), inverse_y.at[y], m_ssem, m_rsem, y_peer(k))
     send_rows(c1, basis[0].astype(BF16), c1_ssem, c1_rsem, z_peer)
+    pass_z()
     send_halo(4, basis)
-    pass_z()
     basis_each = jnp.concatenate([each(t) for t in basis], axis=1)
     halo_r0 = get_halo(0)
     solver_copy.wait()

time: 58.6 us -> 58.8 us (level)
  no operation moved by 1% of the time
where the time goes in v11:
time: 58.8 us; the launch traced here: 58.6 us
  Pallas kernels  56.7 us (96%)
  between operations  1.28 us (2%)
  local copies, waits for them, and re-layouts  0.63 us (1%)
    pallas_call x1, Pallas kernels, on_device(): pl.pallas_call(body, name='schwarz_steps', out_shape=pltpu.VMEM((2,) + ri...  56.7 us

profile of v11, /device:TPU:1, one launch (start us, length us, event | category | flops | bytes accessed | tf_op | source)
XLA Modules:
  0.0 58.6 jit_solution(6186810264962673117)
XLA Ops:
  1.3 56.7 %schwarz_steps.1 = f32[2,16,4,128]{3,2,1,0:T(4,128)S(1)} custom-call(f32[16,4,128]{2,1,0:T(4,128)} %rhs_hbm.1, f32[4,128]{1,0:T(4,128)} %mass_hbm.1, f32[1,128]{1,0:T(1,128)} %bw_hbm.1, s32[1]{0:T(128)S(6)} %copy.9.shift_ref, bf16[16,4,128]{2,1,0:T(4,128)(2,1)} %basis_hbm.1, bf16[1,780,512]{2,1,0:T(8,128)(2,1)} %bitcast.5, bf16[16,8192]{1,0:T(8,128)(2,1)} %inverse_hbm.1), custom_call_target="tpu_custom_call" | custom-call | tf_op jit(solution)/shard_map/schwarz_steps/pallas_call | solution.py:452
  58.0 0.6 %slice_bitcast_fusion = (f32[16,4,128]{2,1,0:T(4,128)}, f32[16,4,128]{2,1,0:T(4,128)}) fusion(f32[2,16,4,128]{3,2,1,0:T(4,128)S(1)} %schwarz_steps.1), kind=kLoop, calls=%fused_computation | loop fusion | bytes 131072 | tf_op jit(solution)/shard_map/squeeze | solution.py:502
